TPU v7x, 256 devices: a whole 4x4x8 slice. The times are simulated.
256 devices in a mesh: dp: 32 (over y, z_hi, core), tensor: 8 (over z_lo, x).
Axes of the slice: x: 4, y: 4, z: 8 (z_hi: 4, z_lo: 2; z = z_hi * 2 + z_lo), core: 2. Of those that a mesh axis runs over, the one named last changes fastest.
Arguments:
- attended: bfloat16 [8192, 6144], P('dp', 'tensor'), may hold values from -6 to 6
- out_weight: bfloat16 [6144, 6144], P('tensor'), may hold values from -0.078125 to 0.078125
- encoder: bfloat16 [6144, 768], P('tensor'), may hold values from -0.078125 to 0.078125
- decoder: bfloat16 [768, 6144], P(None, 'tensor'), may hold values from -0.21875 to 0.21875
- grad_out: bfloat16 [8192, 6144], P('dp', 'tensor'), may hold values from -6 to 6
Outputs:
- decoded: bfloat16 [8192, 6144], P('dp', 'tensor')
- grad_attended: bfloat16 [8192, 6144], P('dp', 'tensor')
- grad_weight: float32 [6144, 6144], P('tensor', 'dp')
- grad_encoder: float32 [6144, 768], P('tensor', 'dp')
- grad_decoder: float32 [768, 6144], P('dp', 'tensor')
All inputs are finite; a program needn't handle non-finite values.
Results may differ from a plain program's by a relative error of at most 0.025.
Values may be sent and summed in bfloat16 or wider, within the bound.
A program may use at most 128 MiB of HBM per device.

v0:
```python
import jax
import jax.numpy as jnp
from jax import lax
from jax.sharding import PartitionSpec as P


def split_halves(values):
    upper = values.astype(jnp.bfloat16)
    lower = (values - upper.astype(jnp.float32)).astype(jnp.bfloat16)
    return (upper, lower)


def split_product(values, right, contract):
    upper, lower = split_halves(values)
    dims = (((contract,), (0,)), ((), ()))
    first = lax.dot_general(upper, right, dims, preferred_element_type=jnp.float32)
    second = lax.dot_general(lower, right, dims, preferred_element_type=jnp.float32)
    return first + second


def body(attended, out_weight, encoder, decoder, grad_out):
    all_tokens = attended.shape[0] * lax.axis_size("dp")
    grad_scale = 1.0 / float(all_tokens) ** 0.5
    partial_value = jnp.dot(attended, out_weight, preferred_element_type=jnp.float32).astype(
        jnp.bfloat16
    )
    whole_encoder = lax.all_gather(encoder, "tensor", axis=0, tiled=True)
    encoded_term = jnp.dot(partial_value, whole_encoder, preferred_element_type=jnp.float32)
    encoded = lax.psum(encoded_term, "tensor")
    code_word = encoded.astype(jnp.bfloat16)
    decoded = jnp.dot(code_word, decoder, preferred_element_type=jnp.float32).astype(jnp.bfloat16)
    code_term = jnp.dot(grad_out, decoder.T, preferred_element_type=jnp.float32)
    grad_code = lax.psum(code_term, "tensor").astype(jnp.bfloat16)
    grad_partial = jnp.dot(grad_code, whole_encoder.T, preferred_element_type=jnp.float32).astype(
        jnp.bfloat16
    )
    summed = lax.psum_scatter(
        partial_value.astype(jnp.float32).astype(jnp.bfloat16),
        "tensor",
        scatter_dimension=1,
        tiled=True,
    ).astype(jnp.float32)
    grad_attended = jnp.dot(grad_partial, out_weight.T, preferred_element_type=jnp.float32).astype(
        jnp.bfloat16
    )
    weight_term = grad_scale * jnp.dot(attended.T, grad_partial, preferred_element_type=jnp.float32)
    grad_weight = lax.psum_scatter(
        weight_term.astype(jnp.bfloat16), "dp", scatter_dimension=1, tiled=True
    ).astype(jnp.float32)
    encoder_term = grad_scale * split_product(summed, grad_code, 0)
    decoder_term = grad_scale * jnp.dot(code_word.T, grad_out, preferred_element_type=jnp.float32)
    grad_encoder, grad_decoder = (
        lax.psum_scatter(
            encoder_term.astype(jnp.bfloat16), "dp", scatter_dimension=1, tiled=True
        ).astype(jnp.float32),
        lax.psum_scatter(
            decoder_term.astype(jnp.bfloat16), "dp", scatter_dimension=0, tiled=True
        ).astype(jnp.float32),
    )
    return (decoded, grad_attended, grad_weight, grad_encoder, grad_decoder)


def solution(mesh):
    placed = (
        P("dp", "tensor"),
        P("tensor", None),
        P("tensor", None),
        P(None, "tensor"),
        P("dp", "tensor"),
    )
    return jax.shard_map(
        body,
        mesh=mesh,
        in_specs=placed,
        out_specs=(
            P("dp", "tensor"),
            P("dp", "tensor"),
            P("tensor", "dp"),
            P("tensor", "dp"),
            P("dp", "tensor"),
        ),
        check_vma=False,
    )
```

profile of v0, /device:TPU:1, one launch (start us, length us, event | category | flops | bytes accessed | tf_op | source)
XLA Modules:
  0.0 521.0 jit_solution(16594927581030184699)
XLA Ops:
  7.2 0.7 all-gather.2.cloned.1.call-update
  8.0 8.1 %convolution_convert_fusion.1 = bf16[256,6144]{1,0:T(8,128)(2,1)} fusion(bf16[256,768]{1,0:T(8,128)(2,1)} %param.5, bf16[768,6144]{1,0:T(8,128)(2,1)} %param.6), kind=kOutput, calls=%fused_computation.3 | convolution fusion | flops 2417491968 | bytes 12976128 | tf_op jit(solution)/shard_map/dot_general | solution.py:24
  16.1 0.9 copy-done.2
  17.1 0.5 fusion.8
  17.6 100.4 %all-gather.2.cloned.1.call-done = bf16[6144,768]{1,0:T(8,128)(2,1)} async-done(((bf16[768,768]{1,0:T(8,128)(2,1)}), bf16[6144,768]{1,0:T(8,128)(2,1)}) %all-gather.2.cloned.1.call-update) | async-done | bytes 9437200 | tf_op jit(solution)/shard_map/all_gather | solution.py:27
  118.0 8.2 %fusion.7 = f32[256,768]{1,0:T(8,128)} fusion(bf16[256,6144]{1,0:T(8,128)(2,1)} %convolution_convert_fusion.1, bf16[6144,768]{1,0:T(8,128)(2,1)} %all-gather.2.cloned.1.call-done), kind=kOutput, calls=%fused_computation.15 | convolution fusion | flops 2415919104 | bytes 13369344 | tf_op jit(solution)/shard_map/dot_general | solution.py:28
  126.2 71.4 %all-reduce.2 = (bf16[256,768]{1,0:T(8,128)(2,1)S(1)}, bf16[256,768]{1,0:T(8,128)(2,1)S(1)}) all-reduce(f32[256,768]{1,0:T(8,128)} %fusion.7, f32[256,768]{1,0:T(8,128)S(1)} %fusion.8), channel_id=1, replica_groups=mesh['dp'=32,'tensor'=8] {'tensor'}, use_global_device_ids=true, to_apply=%region_0.0 | all-reduce | flops 393216 | bytes 2359296 | tf_op jit(solution)/shard_map/psum | solution.py:29
  197.5 0.5 multiply_convert_fusion.1
  198.1 1.5 copy.15
  199.7 1.6 fusion.9
  201.2 1.6 multiply_convert_fusion.2
  202.8 0.2 reduce-scatter.7.cloned.1.call-start
  203.1 10.0 %convolution_convert_fusion = bf16[256,6144]{1,0:T(8,128)(2,1)S(1)} fusion(bf16[6144,768]{1,0:T(8,128)(2,1)} %all-gather.2.cloned.1.call-done, bf16[256,768]{1,0:T(8,128)(2,1)S(1)} %get-tuple-element.16), kind=kOutput, calls=%fused_computation.2 | convolution fusion | flops 2417491968 | bytes 12976128 | tf_op jit(solution)/shard_map/dot_general | solution.py:34
  213.1 1.6 copy-done.4
  214.7 5.1 fusion
  219.9 1.2 convolution_convert_fusion.2
  221.1 8.2 %convolution_convert_fusion.3 = bf16[256,768]{1,0:T(8,128)(2,1)} fusion(bf16[256,6144]{1,0:T(8,128)(2,1)} %copy-done.4, bf16[768,6144]{1,0:T(8,128)(2,1)} %param.6), kind=kOutput, calls=%fused_computation.7 | convolution fusion | flops 2416115712 | bytes 12976128 | tf_op jit(solution)/shard_map/dot_general | solution.py:43
  229.2 64.6 %reduce-scatter.13.cloned.1.call-done = bf16[24,768]{1,0:T(8,128)(2,1)} async-done(((bf16[768,768]{1,0:T(8,128)(2,1)}), bf16[24,768]{1,0:T(8,128)(2,1)}) %reduce-scatter.13.cloned.1.call-update) | async-done | bytes 36880
  293.8 0.9 copy.16
  294.7 0.8 copy.13
  295.5 87.6 %reduce-scatter.11.cloned.1.call-done = bf16[768,24]{0,1:T(8,128)(2,1)} async-done(((bf16[768,768]{0,1:T(8,128)(2,1)}), bf16[768,24]{0,1:T(8,128)(2,1)}) %reduce-scatter.11.cloned.1.call-update) | async-done | bytes 36880 | tf_op jit(solution)/shard_map/reduce_scatter | solution.py:53
  383.2 1.4 convert_element_type.61
  384.6 128.1 %reduce-scatter.7.cloned.1.call-done = bf16[768,192]{0,1:T(8,128)(2,1)} async-done(((bf16[768,6144]{0,1:T(8,128)(2,1)}), bf16[768,192]{0,1:T(8,128)(2,1)}) %reduce-scatter.7.cloned.1.call-update) | async-done | bytes 294928 | tf_op jit(solution)/shard_map/reduce_scatter | solution.py:47
  512.6 1.8 convert_element_type.57
  (17 shorter events, 0.3 us)
Async XLA Ops:
  7.2 9.0 %copy-start = (bf16[768,768]{1,0:T(8,128)(2,1)S(1)}, bf16[768,768]{1,0:T(8,128)(2,1)}, u32[]{:S(2)}) copy-start(bf16[768,768]{1,0:T(8,128)(2,1)} %param.8) | copy-start | bytes 3538948
  7.2 110.8 %all-gather.2.cloned.1.call-start = ((), (), s32[]{:S(2)}) async-start(), calls=%async_computation.4 | async-start | bytes 10616832 | tf_op jit(solution)/shard_map/all_gather | solution.py:27
  7.9 191.7 %reduce-scatter.9.cloned.1.call-start = ((), (), s32[]{:S(2)}) async-start(), calls=%async_computation.6 | async-start | bytes 3538944 | tf_op jit(solution)/shard_map/reduce_scatter | solution.py:37
  16.1 1.0 copy-start.2
  16.1 277.7 %reduce-scatter.13.cloned.1.call-start = ((), (), s32[]{:S(2)}) async-start(), calls=%async_computation.8 | async-start | bytes 1216512
  199.6 183.6 %reduce-scatter.11.cloned.1.call-start = ((), (), s32[]{:S(2)}) async-start(), calls=%async_computation.7 | async-start | bytes 1216512 | tf_op jit(solution)/shard_map/reduce_scatter | solution.py:53
  199.6 1.6 copy-start.1
  202.8 11.9 %copy-start.3 = (bf16[256,768]{1,0:T(8,128)(2,1)S(1)}, bf16[256,768]{1,0:T(8,128)(2,1)}, u32[]{:S(2)}) copy-start(bf16[256,768]{1,0:T(8,128)(2,1)} %param.5) | copy-start | bytes 1179652
  202.8 309.8 %reduce-scatter.7.cloned.1.call-start = ((), (), s32[]{:S(2)}) async-start(), calls=%async_computation.5 | async-start | bytes 9732096 | tf_op jit(solution)/shard_map/reduce_scatter | solution.py:47
  213.1 1.7 copy-start.4
Sparse Core Ops, SparseCore 0:
  9.8 108.1 all-gather.1
  120.5 61.3 reduce-scatter.8
  199.7 94.0 reduce-scatter.12
  297.5 85.5 reduce-scatter.10
  387.0 125.5 reduce-scatter.6
where the time goes:
time: 521 us
  waiting for transfers between devices  381 us (73%)
  blocking collectives  71.4 us (14%)
  matrix products  44.9 us (9%)
  between operations  13.9 us (3%)
  local copies, waits for them, and re-layouts  5.75 us (1%)
    reduce_scatter x1, waiting for transfers between devices, body(): lax.psum_scatter(weight_term.astype(jnp.bfloat16), 'dp', scatter_dimensio...  128 us
    all_gather x1, waiting for transfers between devices, body(): whole_encoder = lax.all_gather(encoder, 'tensor', axis=0, tiled=True)  100 us
    reduce_scatter x1, waiting for transfers between devices, body(): lax.psum_scatter(encoder_term.astype(jnp.bfloat16), 'dp', scatter_dimensi...  87.6 us
    psum x1, blocking collectives, body(): encoded = lax.psum(encoded_term, 'tensor')  71.4 us
    unnamed x6, waiting for transfers between devices  65.3 us
  transfers between devices with their start and end apart: 5, of which 4 were waited for; matrix products, arithmetic and copies ran while one was open for 9% of the time, Pallas kernels for 0%

commit v1 on v0

v1 whole, which is shorter than its diff:
```python
import jax
import jax.numpy as jnp
from jax import lax
from jax.experimental import pallas as pl
from jax.experimental.pallas import tpu as pltpu
from jax.sharding import PartitionSpec as P

MESH = pl.DeviceIdType.MESH
F32 = jnp.float32
BF16 = jnp.bfloat16
TOK = 256
W = 768
H = W // 2
NY, NZ, NT = 4, 4, 8
YB = W // NY
ZB = YB // NZ
CB = ZB // 2
TB = TOK // NT
ER = W // 4
SCALE = 1.0 / float(8192) ** 0.5
N_COPIES = 96


def mm(a, b, ca, cb):
    return lax.dot_general(a, b, (((ca,), (cb,)), ((), ())), preferred_element_type=F32)


def kernel(
    att_h, w_h, enc_h, dec_h, go_h,
    dec_out, ga_out, gw_out, ge_out, gd_out,
    att, wv, enc, dec, go,
    gcs, gcr, gcc, gcf, gct,
    etr, kacc, ksnd, krcv, kt,
    mown, moth, mrcv, mya, myr, myb, myra, myrr, myrb, ms2,
    mza, mzr, mzb, mzra, mzrr, mzrb, mch, mt,
    gs, gr, gsum, gswp, ge_v,
    cws, cwr, cwc, cwf, cwt,
    down, doth, drcv, dya, dyr, dyb, dyra, dyrr, dyrb, ds2,
    dza, dzr, dzb, dzra, dzrr, dzrb, dsum, dswp, gd_v,
    erow, dec_v, ga_v, gw_v,
    lsem, ssem, rsem,
):
    d = lax.axis_index("dp")
    t = lax.axis_index("tensor")
    y, z, c = d // 8, (d // 2) % 4, d % 2
    zl, x = t // 4, t % 4
    sgn = 1 - 2 * c

    def dp_dev(yy, zz, cc):
        return {"dp": ((yy + 4) % 4 * 4 + (zz + 4) % 4) * 2 + cc}

    other = dp_dev(y, z, 1 - c)
    y_next, y_prev = dp_dev(y + sgn, z, c), dp_dev(y - sgn, z, c)
    z_next, z_prev = dp_dev(y, z + sgn, c), dp_dev(y, z - sgn, c)

    def t_to(k):
        kz, kx = k // 4, k % 4
        return (1 - zl if kz else zl) * 4 + (x + kx) % 4

    def t_from(k):
        kz, kx = k // 4, k % 4
        return (1 - zl if kz else zl) * 4 + (x + 4 - kx) % 4

    order = (1, 3, 4, 5, 7, 2, 6)

    def half(cc):
        return pl.ds(pl.multiple_of(cc * H, 128), H)

    def rows(i, n):
        return pl.ds(pl.multiple_of(i * n, n), n)

    me_h, ot_h = half(c), half(1 - c)
    zrow = rows(y * 4 + z, ZB)

    counter = [0]
    sent = []

    def remote(src, dst, dev):
        i = counter[0]
        counter[0] += 1
        cp = pltpu.make_async_remote_copy(
            src_ref=src, dst_ref=dst, send_sem=ssem.at[i], recv_sem=rsem.at[i],
            device_id=dev, device_id_type=MESH,
        )
        return cp

    def send(src, dst, dev):
        cp = remote(src, dst, dev)
        cp.start()
        sent.append(cp)
        return cp

    lcount = [0]

    def local(src, dst):
        i = lcount[0]
        lcount[0] += 1
        cp = pltpu.make_async_copy(src, dst, lsem.at[i])
        cp.start()
        return cp

    l_go = local(go_h, go)
    l_dec = local(dec_h, dec)
    l_enc = local(enc_h, enc)
    l_w = []
    for i in range(NT):
        cols = pl.ds(pl.multiple_of(i * W + c * H, 128), H)
        l_w.append(local(w_h.at[:, cols], wv.at[i]))
    l_att = local(att_h, att)

    barrier = pltpu.get_barrier_semaphore()
    partners = [{"tensor": t_to(k)} for k in order] + [other, y_next, y_prev, z_next, z_prev]
    for dev in partners:
        pl.semaphore_signal(barrier, inc=1, device_id=dev, device_id_type=MESH)

    l_enc.wait()
    pick = (
        lax.broadcasted_iota(jnp.int32, (ZB, W), 1)
        == lax.broadcasted_iota(jnp.int32, (ZB, W), 0) + (y * 4 + z) * ZB
    )
    pick = jnp.where(pick, 1.0, 0.0).astype(BF16)
    etr[0] = mm(pick, enc[rows(c, H), :], 1, 1).astype(BF16)
    l_go.wait()
    l_dec.wait()
    gcs[...] = mm(go[...], dec[...], 1, 1).astype(BF16)

    pl.semaphore_wait(barrier, len(partners))

    et_in = {k: send(etr.at[0], etr.at[k], {"tensor": t_to(k)}) for k in order}
    gc_in = {
        k: send(gcs.at[rows(t_to(k), TB), :], gcr.at[k], {"tensor": t_to(k)}) for k in order
    }

    t_own = d // 4
    rx, rz = (x + 4 - t_own % 4) % 4, (zl + t_own // 4) % 2
    is_own = jnp.logical_and(rx == 0, rz == 0)
    is_two = jnp.logical_and(rx == 0, rz == 1)
    is_three = rx % 2 == 1
    is_last = rx == 2
    passes_on = rx == 1 + 2 * c
    e_recv = counter[0]
    counter[0] += 1
    e_send = [counter[0] + i for i in range(4)]
    counter[0] += 4

    def e_copy(i, dev):
        return pltpu.make_async_remote_copy(
            src_ref=erow, dst_ref=erow, send_sem=ssem.at[e_send[i]], recv_sem=rsem.at[e_recv],
            device_id={"tensor": dev}, device_id_type=MESH,
        )

    e_z = e_copy(0, (1 - zl) * 4 + x)
    e_p = e_copy(1, zl * 4 + (x + 1) % 4)
    e_m = e_copy(2, zl * 4 + (x + 3) % 4)
    e_f = e_copy(3, zl * 4 + (x + 4 + sgn) % 4)

    @pl.when(is_own)
    def _():
        erow[...] = enc[rows(d % 4, ER), :]
        e_z.start()
        e_p.start()
        e_m.start()

    total = None
    for k in (0,) + order:
        if k:
            et_in[k].wait_recv()
        else:
            for cp in l_w:
                cp.wait()
        term = mm(etr[k], wv[t_from(k)], 1, 1)
        total = term if total is None else total + term
    kacc[...] = total
    ksnd[...] = kacc[:, ot_h].astype(BF16)
    k_core = send(ksnd, krcv, other)

    def chunk_sum(own, recv, copies):
        acc = own[rows(t, TB), :].astype(F32)
        for k in order:
            copies[k].wait_recv()
            acc = acc + recv[k].astype(F32)
        return acc.astype(BF16)

    gcc[...] = chunk_sum(gcs, gcr, gc_in)
    gcf[rows(t, TB), :] = gcc[...]
    gcf_in = {k: send(gcc, gcf.at[rows(t, TB), :], {"tensor": t_to(k)}) for k in order}

    def gather_start(buf, row0, n, nxt, prv):
        blk = buf.at[row0, me_h]
        a = send(blk, blk, nxt)
        b = send(blk, blk, prv)
        return a, b

    def z_rows(zz):
        return rows(y * 4 + (zz + 4) % 4, ZB)

    def y_rows(yy):
        return rows((yy + 4) % 4, YB)

    k_core.wait_recv()
    kt[zrow, me_h] = (kacc[:, me_h] + krcv[...].astype(F32)).astype(BF16)

    class Gather:
        def __init__(self, buf):
            self.buf = buf
            self.core_in = []

        def push(self, r, dev):
            blk = self.buf.at[r, me_h]
            return send(blk, blk, dev)

        def core(self, r):
            self.core_in.append(self.push(r, other))

        def z_start(self):
            self.a, self.b = self.push(zrow, z_next), self.push(zrow, z_prev)

        def z_mid(self):
            self.a.wait_recv()
            self.f = self.push(z_rows(z - sgn), z_next)

        def z_end(self):
            self.b.wait_recv()
            self.f.wait_recv()

        def y_start(self):
            self.a, self.b = self.push(y_rows(y), y_next), self.push(y_rows(y), y_prev)
            self.core(y_rows(y))

        def y_mid(self):
            self.a.wait_recv()
            self.f = self.push(y_rows(y - sgn), y_next)
            self.core(y_rows(y - sgn))

        def y_end(self):
            self.b.wait_recv()
            self.core(y_rows(y + sgn))
            self.f.wait_recv()
            self.core(y_rows(y + 2 * sgn))

        def finish(self):
            for cp in self.core_in:
                cp.wait_recv()

    kg = Gather(kt)
    kg.z_start()

    class Scatter:
        def __init__(self, lhs_t, right, own, oth, rcv, ya, yr, yb, yra, yrr, yrb, s2, za, zr, zb, zra, zrr, zrb):
            self.lhs_t, self.right, self.own, self.oth, self.rcv = lhs_t, right, own, oth, rcv
            self.yst = (ya, yr, yb, yra, yrr, yrb)
            self.zst = (za, zr, zb, zra, zrr, zrb)
            self.s2 = s2

        def core_start(self):
            for i in range(3):
                r = slice(i * 256, (i + 1) * 256)
                self.oth[r, :] = mm(self.lhs_t[r, :], self.right[:, ot_h], 1, 0).astype(BF16)
            self.cp = send(self.oth, self.rcv, other)
            for i in range(3):
                r = slice(i * 256, (i + 1) * 256)
                self.own[r, :] = mm(self.lhs_t[r, :], self.right[:, me_h], 1, 0)

        def y_term(self, yy):
            r = y_rows(yy)
            return self.own[r, :] + self.rcv[r, :].astype(F32)

        def z_term(self, zz):
            return self.s2[rows((zz + 4) % 4, ZB), :]

        def ring_start(self, term, pos, bufs, nxt, prv):
            a, r, b, ra, rr, rb = bufs
            r[...] = term(pos + 2 * sgn).astype(BF16)
            self.r_in = send(r, rr, nxt)
            a[...] = term(pos - sgn).astype(BF16)
            self.a_in = send(a, ra, prv)

        def ring_mid(self, term, pos, bufs, nxt):
            a, r, b, ra, rr, rb = bufs
            self.r_in.wait_recv()
            b[...] = (term(pos + sgn) + rr[...].astype(F32)).astype(BF16)
            self.b_in = send(b, rb, nxt)

        def ring_end(self, term, pos, bufs):
            a, r, b, ra, rr, rb = bufs
            self.a_in.wait_recv()
            own = term(pos) + ra[...].astype(F32)
            self.b_in.wait_recv()
            return own + rb[...].astype(F32)

        def y_start(self):
            self.cp.wait_recv()
            self.ring_start(self.y_term, y, self.yst, y_next, y_prev)

        def y_mid(self):
            self.ring_mid(self.y_term, y, self.yst, y_next)

        def y_end(self):
            self.s2[...] = self.ring_end(self.y_term, y, self.yst)

        def z_start(self):
            self.ring_start(self.z_term, z, self.zst, z_next, z_prev)

        def z_mid(self):
            self.ring_mid(self.z_term, z, self.zst, z_next)

        def z_end(self):
            return self.ring_end(self.z_term, z, self.zst)

    for k in order:
        gcf_in[k].wait_recv()
    gct[...] = gcf[...].T
    l_att.wait()
    ms = Scatter(gct, att, mown, moth, mrcv, mya, myr, myb, myra, myrr, myrb, ms2, mza, mzr, mzb, mzra, mzrr, mzrb)
    ms.core_start()

    kg.z_mid()
    kg.z_end()
    kg.y_start()
    ms.y_start()

    @pl.when(is_two)
    def _():
        e_z.wait_recv()
        e_p.start()
        e_m.start()

    kg.y_mid()
    ms.y_mid()
    kg.y_end()

    @pl.when(is_three)
    def _():
        e_z.wait_recv()

    @pl.when(passes_on)
    def _():
        e_f.start()

    kg.finish()

    cws[...] = mm(att[...], kt[...], 1, 1).astype(BF16)
    cw_in = {
        k: send(cws.at[rows(t_to(k), TB), :], cwr.at[k], {"tensor": t_to(k)}) for k in order
    }
    ms.y_end()
    ms.z_start()
    ga_v[...] = mm(gcf[...], kt[...], 1, 0).astype(BF16)
    o_ga = local(ga_v, ga_out)
    ms.z_mid()
    cwc[...] = chunk_sum(cws, cwr, cw_in)
    cwf[rows(t, TB), :] = cwc[...]
    cwf_in = {k: send(cwc, cwf.at[rows(t, TB), :], {"tensor": t_to(k)}) for k in order}

    m_block = ms.z_end().astype(BF16)
    mt[zrow, me_h] = m_block
    mch[c] = m_block
    m_core = send(mch.at[c], mch.at[c], other)
    mg = Gather(mt)
    mg.z_start()

    for k in order:
        cwf_in[k].wait_recv()
    cwt[...] = cwf[...].T
    ds = Scatter(cwt, go, down, doth, drcv, dya, dyr, dyb, dyra, dyrr, dyrb, ds2, dza, dzr, dzb, dzra, dzrr, dzrb)
    ds.core_start()

    mg.z_mid()
    mg.z_end()
    mg.y_start()
    ds.y_start()

    m_core.wait_recv()
    g_in = {}
    for k in order + (0,):
        val = mm(mch[0], wv[t_to(k), :H, :], 1, 0) + mm(mch[1], wv[t_to(k), H:, :], 1, 0)
        if k:
            gs[k] = val.astype(BF16)
            g_in[k] = send(gs.at[k], gr.at[k], {"tensor": t_to(k)})
        else:
            gsum[...] = val

    mg.y_mid()
    ds.y_mid()
    dec_v[...] = mm(cwf[...], dec[...], 1, 0).astype(BF16)
    o_dec = local(dec_v, dec_out)
    mg.y_end()

    for k in order:
        g_in[k].wait_recv()
        gsum[...] += gr[k].astype(F32)
    g_core = send(gsum.at[rows(1 - c, CB), :], gswp, other)

    ds.y_end()
    ds.z_start()

    @pl.when(is_last)
    def _():
        e_z.wait_recv()

    mg.finish()
    gw_v[...] = (SCALE * mm(erow[...], mt[...], 1, 0)).T
    o_gw = local(gw_v, gw_out)

    ds.z_mid()
    g_core.wait_recv()
    ge_v[me_h, :] = (SCALE * gsum[rows(c, CB), :]).T
    ge_v[ot_h, :] = (SCALE * gswp[...]).T
    o_ge = local(ge_v, ge_out)

    dsum[...] = ds.z_end()
    d_core = send(dsum.at[rows(1 - c, CB), :], dswp, other)
    gd_v[:, me_h] = SCALE * dsum[rows(c, CB), :]
    d_core.wait_recv()
    gd_v[:, ot_h] = SCALE * dswp[...]
    o_gd = local(gd_v, gd_out)

    for cp in sent:
        cp.wait_send()

    @pl.when(is_own)
    def _():
        e_z.wait_send()

    @pl.when(rx == 0)
    def _():
        e_p.wait_send()
        e_m.wait_send()

    @pl.when(passes_on)
    def _():
        e_f.wait_send()

    for cp in (o_ga, o_dec, o_gw, o_ge, o_gd):
        cp.wait()
    assert counter[0] <= N_COPIES, counter


def ring_scratch(n):
    return [pltpu.VMEM((n, H), BF16)] * 6


def scatter_scratch():
    return (
        [pltpu.VMEM((W, H), F32), pltpu.VMEM((W, H), BF16), pltpu.VMEM((W, H), BF16)]
        + ring_scratch(YB)
        + [pltpu.VMEM((YB, H), F32)]
        + ring_scratch(ZB)
    )


def body(attended, out_weight, encoder, decoder, grad_out):
    v = pltpu.VMEM
    scratch = (
        [v((TOK, W), BF16), v((NT, W, H), BF16), v((W, W), BF16), v((W, W), BF16), v((TOK, W), BF16)]
        + [v((TOK, W), BF16), v((NT, TB, W), BF16), v((TB, W), BF16), v((TOK, W), BF16), v((W, TOK), BF16)]
        + [v((NT, ZB, H), BF16), v((ZB, W), F32), v((ZB, H), BF16), v((ZB, H), BF16), v((W, W), BF16)]
        + scatter_scratch()
        + [v((2, ZB, H), BF16), v((W, W), BF16)]
        + [v((NT, ZB, H), BF16), v((NT, ZB, H), BF16), v((ZB, H), F32), v((CB, H), F32), v((W, CB), F32)]
        + [v((TOK, W), BF16), v((NT, TB, W), BF16), v((TB, W), BF16), v((TOK, W), BF16), v((W, TOK), BF16)]
        + scatter_scratch()
        + [v((ZB, H), F32), v((CB, H), F32), v((CB, W), F32)]
        + [v((ER, W), BF16), v((TOK, W), BF16), v((TOK, W), BF16), v((W, ER), F32)]
        + [
            pltpu.SemaphoreType.DMA((20,)),
            pltpu.SemaphoreType.DMA((N_COPIES,)),
            pltpu.SemaphoreType.DMA((N_COPIES,)),
        ]
    )
    hbm = pl.BlockSpec(memory_space=pl.ANY)
    return pl.pallas_call(
        kernel,
        out_shape=(
            jax.ShapeDtypeStruct((TOK, W), BF16),
            jax.ShapeDtypeStruct((TOK, W), BF16),
            jax.ShapeDtypeStruct((W, ER), F32),
            jax.ShapeDtypeStruct((W, CB), F32),
            jax.ShapeDtypeStruct((CB, W), F32),
        ),
        in_specs=[hbm] * 5,
        out_specs=[hbm] * 5,
        scratch_shapes=scratch,
        compiler_params=pltpu.CompilerParams(
            collective_id=0, has_side_effects=True, vmem_limit_bytes=48 * 1024 * 1024
        ),
    )(attended, out_weight, encoder, decoder, grad_out)


def solution(mesh):
    return jax.shard_map(
        body,
        mesh=mesh,
        in_specs=(
            P("dp", "tensor"),
            P("tensor", None),
            P("tensor", None),
            P(None, "tensor"),
            P("dp", "tensor"),
        ),
        out_specs=(
            P("dp", "tensor"),
            P("dp", "tensor"),
            P("tensor", "dp"),
            P("tensor", "dp"),
            P("dp", "tensor"),
        ),
        check_vma=False,
    )
```

time: 521 us -> 98.6 us (0.19)
  waiting for transfers between devices: 381 us -> 0 us
  Pallas kernels: 0 us -> 89.2 us
  blocking collectives: 71.4 us -> 0 us
  matrix products: 44.9 us -> 0 us
  between operations: 13.9 us -> 0.65 us
    reduce_scatter x3 -> x0, waiting for transfers between devices: 216 us -> none  [the longest x1 128 us: body(): lax.psum_scatter(weight_term.astype(jnp.bfloat16), 'dp', scatter_dimensio...]
    all_gather x1 -> x0, waiting for transfers between devices: 100 us -> none  [body(): whole_encoder = lax.all_gather(encoder, 'tensor', axis=0, tiled=True)]
    pallas_call x0 -> x1, Pallas kernels: none -> 89.2 us  [body(): pl.pallas_call(kernel, out_shape=(jax.ShapeDtypeStruct((TOK, W), BF16), j...]
    psum x1 -> x0, blocking collectives: 71.4 us -> none  [body(): encoded = lax.psum(encoded_term, 'tensor')]
    unnamed x6 -> x0, waiting for transfers between devices: 65.3 us -> none
    dot_general x10 -> x0, matrix products: 44.9 us -> none  [the longest x1 9.99 us: body(): jnp.dot(grad_code, whole_encoder.T, preferred_element_type=jnp.float32)]
  transfers between devices with their start and end apart: 5 -> 0, of which waited for: 4 -> 0; matrix products, arithmetic and copies ran while one was open for 9% -> 0% of each run, Pallas kernels for 0% -> 0%
where the time goes in v1:
time: 98.6 us; the launch traced here: 98.4 us
  Pallas kernels  89.2 us (90%)
  local copies, waits for them, and re-layouts  8.49 us (9%)
    pallas_call x1, Pallas kernels, body(): pl.pallas_call(kernel, out_shape=(jax.ShapeDtypeStruct((TOK, W), BF16), j...  89.2 us
    unnamed x11, local copies, waits for them, and re-layouts  6.65 us

profile of v1, /device:TPU:1, one launch (start us, length us, event | category | flops | bytes accessed | tf_op | source)
XLA Modules:
  0.0 98.4 jit_solution(12837228641305908853)
XLA Ops:
  0.6 0.0 copy-start
  0.6 1.3 %copy-done = bf16[768,768]{1,0:T(8,128)(2,1)S(1)} copy-done((bf16[768,768]{1,0:T(8,128)(2,1)S(1)}, bf16[768,768]{1,0:T(8,128)(2,1)}, u32[]{:S(2)}) %copy-start) | copy-done | bytes 1179672
  1.9 0.0 copy-start.1
  1.9 1.3 %copy-done.1 = bf16[768,768]{1,0:T(8,128)(2,1)S(1)} copy-done((bf16[768,768]{1,0:T(8,128)(2,1)S(1)}, bf16[768,768]{1,0:T(8,128)(2,1)}, u32[]{:S(2)}) %copy-start.1) | copy-done | bytes 1179672
  3.2 0.0 copy-start.2
  3.2 1.0 %copy-done.2 = bf16[256,768]{1,0:T(8,128)(2,1)S(1)} copy-done((bf16[256,768]{1,0:T(8,128)(2,1)S(1)}, bf16[256,768]{1,0:T(8,128)(2,1)}, u32[]{:S(2)}) %copy-start.2) | copy-done | bytes 393240
  4.2 0.0 copy-start.3
  4.2 1.0 %copy-done.3 = bf16[256,768]{1,0:T(8,128)(2,1)S(1)} copy-done((bf16[256,768]{1,0:T(8,128)(2,1)S(1)}, bf16[256,768]{1,0:T(8,128)(2,1)}, u32[]{:S(2)}) %copy-start.3) | copy-done | bytes 393240
  5.2 89.2 %shard_map.92 = (bf16[256,768]{1,0:T(8,128)(2,1)S(1)}, bf16[256,768]{1,0:T(8,128)(2,1)S(1)}, f32[768,192]{1,0:T(8,128)S(1)}, f32[768,24]{1,0:T(8,128)S(1)}, f32[24,768]{1,0:T(8,128)S(1)}) custom-call(bf16[256,768]{1,0:T(8,128)(2,1)S(1)} %copy-done.2, bf16[768,6144]{1,0:T(8,128)(2,1)} %w_h.1, bf16[768,768]{1,0:T(8,128)(2,1)S(1)} %copy-done, ...), custom_call_target="tpu_custom_call" | custom-call | tf_op jit(solution)/shard_map/pallas_call | solution.py:472
  94.4 0.8 copy.11
  95.2 1.1 %copy.10 = f32[768,192]{0,1:T(8,128)} copy(f32[768,192]{1,0:T(8,128)S(1)} %get-tuple-element.7) | data formatting | bytes 1179648 | tf_op jit(solution)/shard_map/pallas_call | solution.py:472
  96.3 0.7 copy.15
  97.0 0.7 copy.16
  97.7 0.6 copy.17
Async XLA Ops:
  0.6 1.3 %copy-start = (bf16[768,768]{1,0:T(8,128)(2,1)S(1)}, bf16[768,768]{1,0:T(8,128)(2,1)}, u32[]{:S(2)}) copy-start(bf16[768,768]{1,0:T(8,128)(2,1)} %enc_h.1) | copy-start | bytes 3538948
  1.9 1.3 %copy-start.1 = (bf16[768,768]{1,0:T(8,128)(2,1)S(1)}, bf16[768,768]{1,0:T(8,128)(2,1)}, u32[]{:S(2)}) copy-start(bf16[768,768]{1,0:T(8,128)(2,1)} %dec_h.1) | copy-start | bytes 3538948
  3.2 1.0 %copy-start.2 = (bf16[256,768]{1,0:T(8,128)(2,1)S(1)}, bf16[256,768]{1,0:T(8,128)(2,1)}, u32[]{:S(2)}) copy-start(bf16[256,768]{1,0:T(8,128)(2,1)} %att_h.1) | copy-start | bytes 1179652
  4.2 1.0 %copy-start.3 = (bf16[256,768]{1,0:T(8,128)(2,1)S(1)}, bf16[256,768]{1,0:T(8,128)(2,1)}, u32[]{:S(2)}) copy-start(bf16[256,768]{1,0:T(8,128)(2,1)} %go_h.1) | copy-start | bytes 1179652

commit v2 on v1

v2 whole, which is shorter than its diff:
```python
import jax
import jax.numpy as jnp
from jax import lax
from jax.experimental import pallas as pl
from jax.experimental.pallas import tpu as pltpu
from jax.sharding import PartitionSpec as P

MESH = pl.DeviceIdType.MESH
F32 = jnp.float32
BF16 = jnp.bfloat16
TOK = 256
W = 768
H = W // 2
NY, NZ, NT = 4, 4, 8
YB = W // NY
ZB = YB // NZ
CB = ZB // 2
TB = TOK // NT
ER = W // 4
SCALE = 1.0 / float(8192) ** 0.5
N_COPIES = 140
VMEM_LIMIT = 62 * 1024 * 1024


def mm(a, b, ca, cb):
    return lax.dot_general(a, b, (((ca,), (cb,)), ((), ())), preferred_element_type=F32)


def kernel(
    att_h, w_h, enc_h, dec_h, go_h,
    dec_out, ga_out, gw_out, ge_out, gd_out,
    att, wv, enc, dec, go,
    gcs, gcr, gcc, gcf, gct,
    etr, kacc, ksnd, krcv, kt,
    m0, m1, m2, m3, m4, m5, m6, m7, mch, mt,
    gs, gr, gsum, gswp, ge_v,
    cws, cwr, cwc, cwf, cwt,
    d0, d1, d2, d3, d4, d5, d6, d7, dsum, dswp, gd_v,
    erow, dec_v, ga_v, gw_v,
    lsem, ssem, rsem,
):
    d = lax.axis_index("dp")
    t = lax.axis_index("tensor")
    y, z, c = d // 8, (d // 2) % 4, d % 2
    zl, x = t // 4, t % 4
    sgn = 1 - 2 * c

    def dp_dev(yy, zz, cc):
        return {"dp": (yy % 4 * 4 + zz % 4) * 2 + cc}

    other = dp_dev(y, z, 1 - c)

    def y_dev(j):
        return dp_dev(y + j, z, c)

    def z_dev(k):
        return dp_dev(y, z + k, c)

    def t_to(k):
        kz, kx = k // 4, k % 4
        return (1 - zl if kz else zl) * 4 + (x + kx) % 4

    def t_from(k):
        kz, kx = k // 4, k % 4
        return (1 - zl if kz else zl) * 4 + (x + 4 - kx) % 4

    order = (2, 6, 5, 7, 1, 3, 4)
    arrive = (1, 3, 4, 5, 7, 2, 6)

    def half(cc):
        return pl.ds(pl.multiple_of(cc * H, 128), H)

    def rows(i, n):
        return pl.ds(pl.multiple_of(i * n, n), n)

    me_h, ot_h = half(c), half(1 - c)

    def y_rows(yy):
        return rows((yy + 4) % 4, YB)

    def yz_rows(yy, zz):
        return rows((yy + 4) % 4 * 4 + (zz + 4) % 4, ZB)

    counter = [0]
    sent = []

    def remote(src, dst, dev):
        i = counter[0]
        counter[0] += 1
        cp = pltpu.make_async_remote_copy(
            src_ref=src, dst_ref=dst, send_sem=ssem.at[i], recv_sem=rsem.at[i],
            device_id=dev, device_id_type=MESH,
        )
        return cp

    def send(src, dst, dev):
        cp = remote(src, dst, dev)
        cp.start()
        sent.append(cp)
        return cp

    lcount = [0]

    def local(src, dst):
        i = lcount[0]
        lcount[0] += 1
        cp = pltpu.make_async_copy(src, dst, lsem.at[i])
        cp.start()
        return cp

    barrier = pltpu.get_barrier_semaphore()
    partners = (
        [{"tensor": t_to(k)} for k in order]
        + [y_dev(j) for j in (2, 1, 3)]
        + [z_dev(k) for k in (2, 1, 3)]
        + [other]
    )
    for dev in partners:
        pl.semaphore_signal(barrier, inc=1, device_id=dev, device_id_type=MESH)
    l_enc = local(enc_h, enc)
    l_go = local(go_h, go)
    l_dec = local(dec_h, dec)
    l_w = []
    for i in range(NT):
        cols = pl.ds(pl.multiple_of(i * W + c * H, 128), H)
        l_w.append(local(w_h.at[:, cols], wv.at[i]))
    l_att = local(att_h, att)

    l_enc.wait()
    pick = (
        lax.broadcasted_iota(jnp.int32, (ZB, W), 1)
        == lax.broadcasted_iota(jnp.int32, (ZB, W), 0) + (y * 4 + z) * ZB
    )
    pick = jnp.where(pick, 1.0, 0.0).astype(BF16)
    etr[0] = mm(pick, enc[rows(c, H), :], 1, 1).astype(BF16)
    l_go.wait()
    l_dec.wait()
    gcs[...] = mm(go[...], dec[...], 1, 1).astype(BF16)

    pl.semaphore_wait(barrier, len(partners))

    et_in = {k: send(etr.at[0], etr.at[k], {"tensor": t_to(k)}) for k in order}
    gc_in = {
        k: send(gcs.at[rows(t_to(k), TB), :], gcr.at[k], {"tensor": t_to(k)}) for k in order
    }

    t_own = d // 4
    rx, rz = (x + 4 - t_own % 4) % 4, (zl + t_own // 4) % 2
    is_own = jnp.logical_and(rx == 0, rz == 0)
    is_two = jnp.logical_and(rx == 0, rz == 1)
    is_three = rx % 2 == 1
    is_last = rx == 2
    passes_on = rx == 1 + 2 * c
    e_recv = counter[0]
    counter[0] += 1
    e_send = [counter[0] + i for i in range(4)]
    counter[0] += 4

    def e_copy(i, dev):
        return pltpu.make_async_remote_copy(
            src_ref=erow, dst_ref=erow, send_sem=ssem.at[e_send[i]], recv_sem=rsem.at[e_recv],
            device_id={"tensor": dev}, device_id_type=MESH,
        )

    class Tree:
        def __init__(self):
            self.z = e_copy(0, (1 - zl) * 4 + x)
            self.p = e_copy(1, zl * 4 + (x + 1) % 4)
            self.m = e_copy(2, zl * 4 + (x + 3) % 4)
            self.f = e_copy(3, zl * 4 + (x + 4 + sgn) % 4)
            self.at = 0

        def step(self):
            self.at += 1
            if self.at == 1:

                @pl.when(is_own)
                def _():
                    erow[...] = enc[rows(d % 4, ER), :]
                    self.z.start()
                    self.p.start()
                    self.m.start()

            elif self.at == 2:

                @pl.when(is_two)
                def _():
                    self.z.wait_recv()
                    self.p.start()
                    self.m.start()

            elif self.at == 3:

                @pl.when(is_three)
                def _():
                    self.z.wait_recv()

                @pl.when(passes_on)
                def _():
                    self.f.start()

            elif self.at == 4:

                @pl.when(is_last)
                def _():
                    self.z.wait_recv()

        def drain(self):
            if self.at == 0:
                return
            while self.at < 4:
                self.step()

            @pl.when(is_own)
            def _():
                self.z.wait_send()

            @pl.when(rx == 0)
            def _():
                self.p.wait_send()
                self.m.wait_send()

            @pl.when(passes_on)
            def _():
                self.f.wait_send()

    tree = Tree()

    total = None
    for k in (0,) + arrive:
        if k:
            et_in[k].wait_recv()
        else:
            for cp in l_w:
                cp.wait()
        term = mm(etr[k], wv[t_from(k)], 1, 1)
        total = term if total is None else total + term
    kacc[...] = total
    ksnd[...] = kacc[:, ot_h].astype(BF16)
    k_core = send(ksnd, krcv, other)

    def chunk_sum(own, recv, copies):
        acc = own[rows(t, TB), :].astype(F32)
        for k in arrive:
            copies[k].wait_recv()
            acc = acc + recv[k].astype(F32)
        return acc.astype(BF16)

    gcc[...] = chunk_sum(gcs, gcr, gc_in)
    gcf[rows(t, TB), :] = gcc[...]
    gcf_in = {k: send(gcc, gcf.at[rows(t, TB), :], {"tensor": t_to(k)}) for k in order}

    class Gather:
        def __init__(self, buf):
            self.buf = buf
            self.yc = {}
            self.cc = []

        def push(self, r, dev):
            blk = self.buf.at[r, me_h]
            return send(blk, blk, dev)

        def y_send(self, k):
            for j in (2, 1, 3):
                self.yc[k, j] = self.push(yz_rows(y, z - k), y_dev(j))

        def start(self):
            self.zc = {k: self.push(yz_rows(y, z), z_dev(k)) for k in (2, 1, 3)}
            self.y_send(0)

        def z_step(self, k):
            self.zc[k].wait_recv()
            self.y_send(k)

        def z_rest(self):
            for k in (1, 3, 2):
                self.z_step(k)
            self.cc.append(self.push(y_rows(y), other))

        def y_step(self, j):
            for k in (0, 1, 3, 2):
                self.yc[k, j].wait_recv()
            self.cc.append(self.push(y_rows(y - j), other))

        def y_rest(self):
            for j in (1, 3, 2):
                self.y_step(j)

        def finish(self):
            for cp in self.cc:
                cp.wait_recv()

    class Scatter:
        def __init__(self, lhs_t, right, bufs):
            self.lhs_t, self.right = lhs_t, right
            self.own, self.oth, self.rcv, self.ys, self.yr, self.zs, self.zr, self.zown = bufs

        def core_start(self):
            self.cc = {}
            for j in (2, 1, 3, 0):
                r = y_rows(y + j)
                self.oth[r, :] = mm(self.lhs_t[r, :], self.right[:, ot_h], 1, 0).astype(BF16)
                self.cc[j] = send(self.oth.at[r, :], self.rcv.at[r, :], other)
            for j in (2, 1, 3, 0):
                r = y_rows(y + j)
                self.own[r, :] = mm(self.lhs_t[r, :], self.right[:, me_h], 1, 0)

        def y_start(self):
            self.yc = {}
            for j in (2, 1, 3):
                r = y_rows(y + j)
                self.cc[j].wait_recv()
                self.ys[j - 1] = (self.own[r, :] + self.rcv[r, :].astype(F32)).astype(BF16)
            for k in (2, 1, 3, 0):
                r = rows((z + k) % 4, ZB)
                for j in (2, 1, 3):
                    self.yc[k, j] = send(self.ys.at[j - 1, r, :], self.yr.at[j - 1, r, :], y_dev(j))
            self.cc[0].wait_recv()

        def z_start(self):
            self.zc = {}
            for k in (2, 1, 3, 0):
                r = rows((z + k) % 4, ZB)
                yz = yz_rows(y, z + k)
                val = self.own[yz, :] + self.rcv[yz, :].astype(F32)
                for j in (1, 3, 2):
                    self.yc[k, j].wait_recv()
                    val = val + self.yr[j - 1, r, :].astype(F32)
                if k:
                    self.zs[k - 1] = val.astype(BF16)
                    self.zc[k] = send(self.zs.at[k - 1], self.zr.at[k - 1], z_dev(k))
                else:
                    self.zown[...] = val

        def z_end(self):
            val = self.zown[...]
            for k in (1, 3, 2):
                self.zc[k].wait_recv()
                val = val + self.zr[k - 1].astype(F32)
            return val

    k_core.wait_recv()
    kt[yz_rows(y, z), me_h] = (kacc[:, me_h] + krcv[...].astype(F32)).astype(BF16)
    kg = Gather(kt)
    kg.start()
    kg.z_rest()

    for k in arrive:
        gcf_in[k].wait_recv()
    gct[...] = gcf[...].T
    l_att.wait()
    ms = Scatter(gct, att, (m0, m1, m2, m3, m4, m5, m6, m7))
    ms.core_start()
    ms.y_start()
    tree.step()
    kg.y_rest()
    kg.finish()

    cws[...] = mm(att[...], kt[...], 1, 1).astype(BF16)
    cw_in = {
        k: send(cws.at[rows(t_to(k), TB), :], cwr.at[k], {"tensor": t_to(k)}) for k in order
    }
    ga_v[...] = mm(gcf[...], kt[...], 1, 0).astype(BF16)
    o_ga = local(ga_v, ga_out)
    ms.z_start()
    tree.step()
    cwc[...] = chunk_sum(cws, cwr, cw_in)
    cwf[rows(t, TB), :] = cwc[...]
    cwf_in = {k: send(cwc, cwf.at[rows(t, TB), :], {"tensor": t_to(k)}) for k in order}

    m_block = ms.z_end().astype(BF16)
    mt[yz_rows(y, z), me_h] = m_block
    mch[c] = m_block
    m_core = send(mch.at[c], mch.at[c], other)
    mg = Gather(mt)
    mg.start()

    m_core.wait_recv()
    g_in = {}
    for k in order + (0,):
        val = mm(mch[0], wv[t_to(k), :H, :], 1, 0) + mm(mch[1], wv[t_to(k), H:, :], 1, 0)
        if k:
            gs[k] = val.astype(BF16)
            g_in[k] = send(gs.at[k], gr.at[k], {"tensor": t_to(k)})
        else:
            gsum[...] = val

    tree.step()
    mg.z_rest()
    for k in arrive:
        cwf_in[k].wait_recv()
    cwt[...] = cwf[...].T
    ds = Scatter(cwt, go, (d0, d1, d2, d3, d4, d5, d6, d7))
    ds.core_start()
    ds.y_start()
    dec_v[...] = mm(cwf[...], dec[...], 1, 0).astype(BF16)
    o_dec = local(dec_v, dec_out)
    mg.y_rest()
    for k in arrive:
        g_in[k].wait_recv()
        gsum[...] += gr[k].astype(F32)
    g_core = send(gsum.at[rows(1 - c, CB), :], gswp, other)
    mg.finish()
    tree.step()
    gw_v[...] = SCALE * mm(erow[...], mt[...], 1, 0)
    o_gw = local(gw_v, gw_out)
    g_core.wait_recv()
    ge_v[:, me_h] = SCALE * gsum[rows(c, CB), :]
    ge_v[:, ot_h] = SCALE * gswp[...]
    o_ge = local(ge_v, ge_out)

    ds.z_start()
    dsum[...] = ds.z_end()
    d_core = send(dsum.at[rows(1 - c, CB), :], dswp, other)
    gd_v[:, me_h] = SCALE * dsum[rows(c, CB), :]
    d_core.wait_recv()
    gd_v[:, ot_h] = SCALE * dswp[...]
    o_gd = local(gd_v, gd_out)

    for cp in sent:
        cp.wait_send()
    tree.drain()
    for cp in (o_ga, o_dec, o_gw, o_ge, o_gd):
        cp.wait()
    assert counter[0] <= N_COPIES, counter


def hand_on(*refs):
    ins, outs, held, sem_in, sem_out = refs[:5], refs[5:10], refs[10:15], refs[15], refs[16]
    first = [pltpu.make_async_copy(ins[i], held[i], sem_in.at[i]) for i in range(5)]
    second = [pltpu.make_async_copy(held[i], outs[i], sem_out.at[i]) for i in range(5)]
    for cp in first:
        cp.start()
    for i in (3, 4, 0, 1, 2):
        first[i].wait()
        second[i].start()
    for cp in second:
        cp.wait()


def scatter_scratch():
    v = pltpu.VMEM
    return [
        v((W, H), F32), v((W, H), BF16), v((W, H), BF16), v((3, YB, H), BF16), v((3, YB, H), BF16),
        v((3, ZB, H), BF16), v((3, ZB, H), BF16), v((ZB, H), F32),
    ]


def body(attended, out_weight, encoder, decoder, grad_out):
    v = pltpu.VMEM
    scratch = (
        [v((TOK, W), BF16), v((NT, W, H), BF16), v((W, W), BF16), v((W, W), BF16), v((TOK, W), BF16)]
        + [v((TOK, W), BF16), v((NT, TB, W), BF16), v((TB, W), BF16), v((TOK, W), BF16), v((W, TOK), BF16)]
        + [v((NT, ZB, H), BF16), v((ZB, W), F32), v((ZB, H), BF16), v((ZB, H), BF16), v((W, W), BF16)]
        + scatter_scratch()
        + [v((2, ZB, H), BF16), v((W, W), BF16)]
        + [v((NT, ZB, H), BF16), v((NT, ZB, H), BF16), v((ZB, H), F32), v((CB, H), F32), v((CB, W), F32)]
        + [v((TOK, W), BF16), v((NT, TB, W), BF16), v((TB, W), BF16), v((TOK, W), BF16), v((W, TOK), BF16)]
        + scatter_scratch()
        + [v((ZB, H), F32), v((CB, H), F32), v((CB, W), F32)]
        + [v((ER, W), BF16), v((TOK, W), BF16), v((TOK, W), BF16), v((ER, W), F32)]
        + [
            pltpu.SemaphoreType.DMA((20,)),
            pltpu.SemaphoreType.DMA((N_COPIES,)),
            pltpu.SemaphoreType.DMA((N_COPIES,)),
        ]
    )
    hbm = pl.BlockSpec(memory_space=pl.ANY)
    shapes = (
        jax.ShapeDtypeStruct((TOK, W), BF16),
        jax.ShapeDtypeStruct((TOK, W), BF16),
        jax.ShapeDtypeStruct((ER, W), F32),
        jax.ShapeDtypeStruct((CB, W), F32),
        jax.ShapeDtypeStruct((CB, W), F32),
    )
    results = pl.pallas_call(
        kernel,
        out_shape=shapes,
        in_specs=[hbm] * 5,
        out_specs=[hbm] * 5,
        scratch_shapes=scratch,
        compiler_params=pltpu.CompilerParams(
            collective_id=0, has_side_effects=True, vmem_limit_bytes=VMEM_LIMIT
        ),
    )(attended, out_weight, encoder, decoder, grad_out)
    decoded, grad_attended, weight_t, encoder_t, grad_decoder = pl.pallas_call(
        hand_on,
        out_shape=shapes,
        in_specs=[hbm] * 5,
        out_specs=[hbm] * 5,
        scratch_shapes=[v(a.shape, a.dtype) for a in shapes]
        + [pltpu.SemaphoreType.DMA((5,))] * 2,
        compiler_params=pltpu.CompilerParams(vmem_limit_bytes=VMEM_LIMIT),
    )(*results)
    return decoded, grad_attended, weight_t.T, encoder_t.T, grad_decoder


def solution(mesh):
    return jax.shard_map(
        body,
        mesh=mesh,
        in_specs=(
            P("dp", "tensor"),
            P("tensor", None),
            P("tensor", None),
            P(None, "tensor"),
            P("dp", "tensor"),
        ),
        out_specs=(
            P("dp", "tensor"),
            P("dp", "tensor"),
            P("tensor", "dp"),
            P("tensor", "dp"),
            P("dp", "tensor"),
        ),
        check_vma=False,
    )
```

time: 98.6 us -> 79.7 us (0.81)
  Pallas kernels: 89.2 us -> 78.9 us
  local copies, waits for them, and re-layouts: 8.49 us -> 0 us
    pallas_call x1 -> x2, Pallas kernels: 89.2 us -> 78.9 us  [the longest x1 76.4 us: body(): pl.pallas_call(kernel, out_shape=shapes, in_specs=[hbm] * 5, out_specs=[h...]
    unnamed x11 -> x0, local copies, waits for them, and re-layouts: 6.65 us -> none
    pallas_call x2 -> x0, local copies, waits for them, and re-layouts: 1.84 us -> none  [body(): pl.pallas_call(kernel, out_shape=(jax.ShapeDtypeStruct((TOK, W), BF16), j...]
where the time goes in v2:
time: 79.7 us; the launch traced here: 79.6 us
  Pallas kernels  78.9 us (99%)
    pallas_call x1, Pallas kernels, body(): pl.pallas_call(kernel, out_shape=shapes, in_specs=[hbm] * 5, out_specs=[h...  76.4 us
    pallas_call x1, Pallas kernels, body(): pl.pallas_call(hand_on, out_shape=shapes, in_specs=[hbm] * 5, out_specs=[...  2.51 us

profile of v2, /device:TPU:1, one launch (start us, length us, event | category | flops | bytes accessed | tf_op | source)
XLA Modules:
  0.0 79.6 jit_solution(13348634003441035683)
XLA Ops:
  0.6 76.4 %shard_map.92 = (bf16[256,768]{1,0:T(8,128)(2,1)}, bf16[256,768]{1,0:T(8,128)(2,1)}, f32[192,768]{1,0:T(8,128)}, f32[24,768]{1,0:T(8,128)}, f32[24,768]{1,0:T(8,128)}) custom-call(bf16[256,768]{1,0:T(8,128)(2,1)} %att_h.1, bf16[768,6144]{1,0:T(8,128)(2,1)} %w_h.1, bf16[768,768]{1,0:T(8,128)(2,1)} %enc_h.1, bf16[768,768]{1,0:T(8,128)(2,1)} %dec_h.1, ...), custom_call_target="tpu_custom_call" | custom-call | tf_op jit(solution)/shard_map/pallas_call | solution.py:476
  77.1 2.5 %shard_map.93 = (bf16[256,768]{1,0:T(8,128)(2,1)}, bf16[256,768]{1,0:T(8,128)(2,1)}, f32[192,768]{1,0:T(8,128)}, f32[24,768]{1,0:T(8,128)}, f32[24,768]{1,0:T(8,128)}) custom-call(bf16[256,768]{1,0:T(8,128)(2,1)} %get-tuple-element.15.refs_0_, bf16[256,768]{1,0:T(8,128)(2,1)} %get-tuple-element.16.refs_1_, f32[192,768]{1,0:T(8,128)} %get-tuple-element.17.refs_2_, ...), custom_call_target="tpu_custom_call" | custom-call | tf_op jit(solution)/shard_map/pallas_call | solution.py:486

commit v3 on v2

--- a/solution.py
+++ b/solution.py
@@ -20,6 +20,16 @@
 SCALE = 1.0 / float(8192) ** 0.5
 N_COPIES = 140
 VMEM_LIMIT = 62 * 1024 * 1024
+T1 = 7
+T2 = 2
+T3 = 3
+NO_TREE = False
+TG = True
+SORD = True
+GCPOS = 2
+MYP = 1
+MZP = 1
+MGP = 1
 
 
 def mm(a, b, ca, cb):
@@ -30,11 +40,11 @@
     att_h, w_h, enc_h, dec_h, go_h,
     dec_out, ga_out, gw_out, ge_out, gd_out,
     att, wv, enc, dec, go,
-    gcs, gcr, gcc, gcf, gct,
+    gcs, gcr, gcf, gct,
     etr, kacc, ksnd, krcv, kt,
     m0, m1, m2, m3, m4, m5, m6, m7, mch, mt,
     gs, gr, gsum, gswp, ge_v,
-    cws, cwr, cwc, cwf, cwt,
+    cws, cwr, cwf, cwt,
     d0, d1, d2, d3, d4, d5, d6, d7, dsum, dswp, gd_v,
     erow, dec_v, ga_v, gw_v,
     lsem, ssem, rsem,
@@ -51,7 +61,7 @@
     other = dp_dev(y, z, 1 - c)
 
     def y_dev(j):
-        return dp_dev(y + j, z, c)
+        return dp_dev(y + j + 4, z, c)
 
     def z_dev(k):
         return dp_dev(y, z + k, c)
@@ -76,10 +86,10 @@
     me_h, ot_h = half(c), half(1 - c)
 
     def y_rows(yy):
-        return rows((yy + 4) % 4, YB)
+        return rows((yy + 8) % 4, YB)
 
     def yz_rows(yy, zz):
-        return rows((yy + 4) % 4 * 4 + (zz + 4) % 4, ZB)
+        return rows((yy + 8) % 4 * 4 + (zz + 8) % 4, ZB)
 
     counter = [0]
     sent = []
@@ -117,14 +127,9 @@
     )
     for dev in partners:
         pl.semaphore_signal(barrier, inc=1, device_id=dev, device_id_type=MESH)
-    l_enc = local(enc_h, enc)
+    l_enc = local(enc_h.at[rows(c, H), :], enc)
     l_go = local(go_h, go)
     l_dec = local(dec_h, dec)
-    l_w = []
-    for i in range(NT):
-        cols = pl.ds(pl.multiple_of(i * W + c * H, 128), H)
-        l_w.append(local(w_h.at[:, cols], wv.at[i]))
-    l_att = local(att_h, att)
 
     l_enc.wait()
     pick = (
@@ -132,17 +137,59 @@
         == lax.broadcasted_iota(jnp.int32, (ZB, W), 0) + (y * 4 + z) * ZB
     )
     pick = jnp.where(pick, 1.0, 0.0).astype(BF16)
-    etr[0] = mm(pick, enc[rows(c, H), :], 1, 1).astype(BF16)
+    etr[t] = mm(pick, enc[...], 1, 1).astype(BF16)
     l_go.wait()
     l_dec.wait()
+    l_w = []
+    for i in range(NT):
+        cols = pl.ds(pl.multiple_of(i * W + c * H, 128), H)
+        l_w.append(local(w_h.at[:, cols], wv.at[i]))
+    l_att = local(att_h, att)
     gcs[...] = mm(go[...], dec[...], 1, 1).astype(BF16)
 
     pl.semaphore_wait(barrier, len(partners))
 
-    et_in = {k: send(etr.at[0], etr.at[k], {"tensor": t_to(k)}) for k in order}
-    gc_in = {
-        k: send(gcs.at[rows(t_to(k), TB), :], gcr.at[k], {"tensor": t_to(k)}) for k in order
-    }
+    class TensorGather:
+        def __init__(self, blk):
+            self.blk = blk
+            self.cp = {}
+
+        def push(self, tt, k):
+            self.cp[k] = send(self.blk(tt), self.blk(tt), {"tensor": t_to(k % 4 if TG else k)})
+
+        def start(self):
+            if not TG:
+                for k in order:
+                    self.push(t, k)
+                return
+            self.cp[4] = send(self.blk(t), self.blk(t), {"tensor": t_to(4)})
+            for k in (2, 1, 3):
+                self.push(t, k)
+
+        def mid(self):
+            if TG:
+                self.cp[4].wait_recv()
+                for k in (6, 5, 7):
+                    self.push(t_to(4), k)
+
+        def end(self, ks=arrive):
+            for k in ks:
+                if not (TG and k == 4):
+                    self.cp[k].wait_recv()
+
+    et = TensorGather(lambda tt: etr.at[tt])
+
+    def gc_send():
+        return {
+            k: send(gcs.at[rows(t_to(k), TB), :], gcr.at[k], {"tensor": t_to(k)}) for k in order
+        }
+
+    et.start()
+    if GCPOS == 0:
+        gc_in = gc_send()
+    et.mid()
+    if GCPOS == 1:
+        gc_in = gc_send()
 
     t_own = d // 4
     rx, rz = (x + 4 - t_own % 4) % 4, (zl + t_own // 4) % 2
@@ -176,7 +223,9 @@
 
                 @pl.when(is_own)
                 def _():
-                    erow[...] = enc[rows(d % 4, ER), :]
+                    cp = pltpu.make_async_copy(enc_h.at[rows(d % 4, ER), :], erow, lsem.at[19])
+                    cp.start()
+                    cp.wait()
                     self.z.start()
                     self.p.start()
                     self.m.start()
@@ -226,18 +275,10 @@
 
     tree = Tree()
 
-    total = None
-    for k in (0,) + arrive:
-        if k:
-            et_in[k].wait_recv()
-        else:
-            for cp in l_w:
-                cp.wait()
-        term = mm(etr[k], wv[t_from(k)], 1, 1)
-        total = term if total is None else total + term
-    kacc[...] = total
-    ksnd[...] = kacc[:, ot_h].astype(BF16)
-    k_core = send(ksnd, krcv, other)
+    def step(at):
+        for i in (T1, T2, T3, 4):
+            if i == at and not NO_TREE:
+                tree.step()
 
     def chunk_sum(own, recv, copies):
         acc = own[rows(t, TB), :].astype(F32)
@@ -246,9 +287,23 @@
             acc = acc + recv[k].astype(F32)
         return acc.astype(BF16)
 
-    gcc[...] = chunk_sum(gcs, gcr, gc_in)
-    gcf[rows(t, TB), :] = gcc[...]
-    gcf_in = {k: send(gcc, gcf.at[rows(t, TB), :], {"tensor": t_to(k)}) for k in order}
+    gcg = TensorGather(lambda tt: gcf.at[rows(tt, TB), :])
+    total = None
+    for k in (0, 4, 1, 3, 2, 5, 7, 6):
+        if k:
+            et.end((k,))
+        else:
+            for cp in l_w:
+                cp.wait()
+        if k == 2 and GCPOS == 2:
+            gc_in = gc_send()
+        term = mm(etr[t_from(k)], wv[t_from(k)], 1, 1)
+        total = term if total is None else total + term
+    kacc[...] = total
+    ksnd[...] = kacc[:, ot_h].astype(BF16)
+    k_core = send(ksnd, krcv, other)
+    if GCPOS == 3:
+        gc_in = gc_send()
 
     class Gather:
         def __init__(self, buf):
@@ -257,7 +312,7 @@
             self.cc = []
 
         def push(self, r, dev):
-            blk = self.buf.at[r, me_h]
+            blk = self.buf.at[c, r]
             return send(blk, blk, dev)
 
         def y_send(self, k):
@@ -275,6 +330,9 @@
         def z_rest(self):
             for k in (1, 3, 2):
                 self.z_step(k)
+            self.own_row()
+
+        def own_row(self):
             self.cc.append(self.push(y_rows(y), other))
 
         def y_step(self, j):
@@ -301,9 +359,15 @@
                 r = y_rows(y + j)
                 self.oth[r, :] = mm(self.lhs_t[r, :], self.right[:, ot_h], 1, 0).astype(BF16)
                 self.cc[j] = send(self.oth.at[r, :], self.rcv.at[r, :], other)
+
+        def core_own(self):
             for j in (2, 1, 3, 0):
                 r = y_rows(y + j)
                 self.own[r, :] = mm(self.lhs_t[r, :], self.right[:, me_h], 1, 0)
+
+        def y_send(self, k, j):
+            r = rows((z + k) % 4, ZB)
+            self.yc[k, j] = send(self.ys.at[j - 1, r, :], self.yr.at[j - 1, r, :], y_dev(j))
 
         def y_start(self):
             self.yc = {}
@@ -311,15 +375,21 @@
                 r = y_rows(y + j)
                 self.cc[j].wait_recv()
                 self.ys[j - 1] = (self.own[r, :] + self.rcv[r, :].astype(F32)).astype(BF16)
+                if SORD and j == 2:
+                    for k in (2, 1, 3, 0):
+                        self.y_send(k, j)
             for k in (2, 1, 3, 0):
-                r = rows((z + k) % 4, ZB)
-                for j in (2, 1, 3):
-                    self.yc[k, j] = send(self.ys.at[j - 1, r, :], self.yr.at[j - 1, r, :], y_dev(j))
+                for j in (1, 3) if SORD else (2, 1, 3):
+                    self.y_send(k, j)
             self.cc[0].wait_recv()
 
         def z_start(self):
             self.zc = {}
             for k in (2, 1, 3, 0):
+                self.z_sum(k)
+
+        def z_sum(self, k):
+            if 1:
                 r = rows((z + k) % 4, ZB)
                 yz = yz_rows(y, z + k)
                 val = self.own[yz, :] + self.rcv[yz, :].astype(F32)
@@ -340,43 +410,89 @@
             return val
 
     k_core.wait_recv()
-    kt[yz_rows(y, z), me_h] = (kacc[:, me_h] + krcv[...].astype(F32)).astype(BF16)
+    kt[c, yz_rows(y, z)] = (kacc[:, me_h] + krcv[...].astype(F32)).astype(BF16)
     kg = Gather(kt)
     kg.start()
-    kg.z_rest()
-
-    for k in arrive:
-        gcf_in[k].wait_recv()
-    gct[...] = gcf[...].T
+    if GCPOS < 2:
+        gcf[rows(t, TB), :] = chunk_sum(gcs, gcr, gc_in)
+        gcg.start()
+        kg.z_step(1)
+        kg.z_step(3)
+        gcg.mid()
+        kg.z_step(2)
+        kg.own_row()
+    else:
+        kg.z_step(1)
+        kg.z_step(3)
+        kg.z_step(2)
+        kg.own_row()
+        step(6)
+        gcf[rows(t, TB), :] = chunk_sum(gcs, gcr, gc_in)
+        gcg.start()
+        gcg.mid()
+    step(7)
+
     l_att.wait()
     ms = Scatter(gct, att, (m0, m1, m2, m3, m4, m5, m6, m7))
-    ms.core_start()
-    ms.y_start()
-    tree.step()
-    kg.y_rest()
+    if MYP == 0:
+        gcg.end()
+        gct[...] = gcf[...].T
+        ms.core_start()
+        ms.core_own()
+        ms.y_start()
+    kg.y_step(1)
+    kg.y_step(3)
+    if MYP >= 1:
+        gcg.end()
+        gct[...] = gcf[...].T
+        ms.core_start()
+    kg.y_step(2)
+    if MYP == 1:
+        ms.core_own()
+    if MYP == 2:
+        ms.core_own()
+        ms.y_start()
     kg.finish()
-
-    cws[...] = mm(att[...], kt[...], 1, 1).astype(BF16)
+    step(0)
+
+    cws[...] = (mm(att[:, :H], kt[0], 1, 1) + mm(att[:, H:], kt[1], 1, 1)).astype(BF16)
     cw_in = {
         k: send(cws.at[rows(t_to(k), TB), :], cwr.at[k], {"tensor": t_to(k)}) for k in order
     }
-    ga_v[...] = mm(gcf[...], kt[...], 1, 0).astype(BF16)
+    if MYP == 1:
+        ms.y_start()
+    ga_v[:, :H] = mm(gcf[...], kt[0], 1, 0).astype(BF16)
+    ga_v[:, H:] = mm(gcf[...], kt[1], 1, 0).astype(BF16)
     o_ga = local(ga_v, ga_out)
-    ms.z_start()
-    tree.step()
-    cwc[...] = chunk_sum(cws, cwr, cw_in)
-    cwf[rows(t, TB), :] = cwc[...]
-    cwf_in = {k: send(cwc, cwf.at[rows(t, TB), :], {"tensor": t_to(k)}) for k in order}
-
+    if MZP == 0:
+        ms.z_start()
+    cwf[rows(t, TB), :] = chunk_sum(cws, cwr, cw_in)
+    cwg = TensorGather(lambda tt: cwf.at[rows(tt, TB), :])
+    cwg.start()
+    if MZP == 1:
+        ms.z_start()
+    cwg.mid()
+    step(1)
+    if MZP == 2:
+        ms.z_start()
     m_block = ms.z_end().astype(BF16)
-    mt[yz_rows(y, z), me_h] = m_block
+    mt[c, yz_rows(y, z)] = m_block
     mch[c] = m_block
     m_core = send(mch.at[c], mch.at[c], other)
     mg = Gather(mt)
     mg.start()
-
+    cwg.end()
+    step(2)
+    cwt[...] = cwf[...].T
+    ds = Scatter(cwt, go, (d0, d1, d2, d3, d4, d5, d6, d7))
+    ds.core_start()
+    ds.core_own()
+    if MGP == 0:
+        mg.z_step(1)
+        mg.z_step(3)
+    ds.y_start()
+    g_in = {}
     m_core.wait_recv()
-    g_in = {}
     for k in order + (0,):
         val = mm(mch[0], wv[t_to(k), :H, :], 1, 0) + mm(mch[1], wv[t_to(k), H:, :], 1, 0)
         if k:
@@ -384,34 +500,38 @@
             g_in[k] = send(gs.at[k], gr.at[k], {"tensor": t_to(k)})
         else:
             gsum[...] = val
-
-    tree.step()
-    mg.z_rest()
-    for k in arrive:
-        cwf_in[k].wait_recv()
-    cwt[...] = cwf[...].T
-    ds = Scatter(cwt, go, (d0, d1, d2, d3, d4, d5, d6, d7))
-    ds.core_start()
-    ds.y_start()
+    step(8)
+    if MGP == 1:
+        mg.z_step(1)
+        mg.z_step(3)
+    mg.z_step(2)
+    mg.own_row()
     dec_v[...] = mm(cwf[...], dec[...], 1, 0).astype(BF16)
     o_dec = local(dec_v, dec_out)
-    mg.y_rest()
+    step(3)
+    ds.zc = {}
+    ds.z_sum(2)
     for k in arrive:
         g_in[k].wait_recv()
         gsum[...] += gr[k].astype(F32)
     g_core = send(gsum.at[rows(1 - c, CB), :], gswp, other)
-    mg.finish()
-    tree.step()
-    gw_v[...] = SCALE * mm(erow[...], mt[...], 1, 0)
-    o_gw = local(gw_v, gw_out)
+    ds.z_sum(1)
+    ds.z_sum(3)
+    ds.z_sum(0)
+    mg.y_step(1)
+    mg.y_step(3)
+    mg.y_step(2)
+    step(4)
     g_core.wait_recv()
     ge_v[:, me_h] = SCALE * gsum[rows(c, CB), :]
     ge_v[:, ot_h] = SCALE * gswp[...]
     o_ge = local(ge_v, ge_out)
-
-    ds.z_start()
     dsum[...] = ds.z_end()
     d_core = send(dsum.at[rows(1 - c, CB), :], dswp, other)
+    mg.finish()
+    gw_v[:, :H] = SCALE * mm(erow[...], mt[0], 1, 0)
+    gw_v[:, H:] = SCALE * mm(erow[...], mt[1], 1, 0)
+    o_gw = local(gw_v, gw_out)
     gd_v[:, me_h] = SCALE * dsum[rows(c, CB), :]
     d_core.wait_recv()
     gd_v[:, ot_h] = SCALE * dswp[...]
@@ -427,13 +547,16 @@
 
 def hand_on(*refs):
     ins, outs, held, sem_in, sem_out = refs[:5], refs[5:10], refs[10:15], refs[15], refs[16]
-    first = [pltpu.make_async_copy(ins[i], held[i], sem_in.at[i]) for i in range(5)]
-    second = [pltpu.make_async_copy(held[i], outs[i], sem_out.at[i]) for i in range(5)]
+    pieces = [(2, slice(i * 64, i * 64 + 64)) for i in range(3)]
+    pieces += [(a, slice(i * 128, i * 128 + 128)) for a in (0, 1) for i in range(2)]
+    pieces += [(a, slice(0, CB)) for a in (3, 4)]
+    first = [pltpu.make_async_copy(ins[a].at[r], held[a].at[r], sem_in.at[i]) for i, (a, r) in enumerate(pieces)]
+    second = [pltpu.make_async_copy(held[a].at[r], outs[a].at[r], sem_out.at[i]) for i, (a, r) in enumerate(pieces)]
     for cp in first:
         cp.start()
-    for i in (3, 4, 0, 1, 2):
-        first[i].wait()
-        second[i].start()
+    for one, two in zip(first, second):
+        one.wait()
+        two.start()
     for cp in second:
         cp.wait()
 
@@ -449,13 +572,13 @@
 def body(attended, out_weight, encoder, decoder, grad_out):
     v = pltpu.VMEM
     scratch = (
-        [v((TOK, W), BF16), v((NT, W, H), BF16), v((W, W), BF16), v((W, W), BF16), v((TOK, W), BF16)]
-        + [v((TOK, W), BF16), v((NT, TB, W), BF16), v((TB, W), BF16), v((TOK, W), BF16), v((W, TOK), BF16)]
-        + [v((NT, ZB, H), BF16), v((ZB, W), F32), v((ZB, H), BF16), v((ZB, H), BF16), v((W, W), BF16)]
+        [v((TOK, W), BF16), v((NT, W, H), BF16), v((H, W), BF16), v((W, W), BF16), v((TOK, W), BF16)]
+        + [v((TOK, W), BF16), v((NT, TB, W), BF16), v((TOK, W), BF16), v((W, TOK), BF16)]
+        + [v((NT, ZB, H), BF16), v((ZB, W), F32), v((ZB, H), BF16), v((ZB, H), BF16), v((2, W, H), BF16)]
         + scatter_scratch()
-        + [v((2, ZB, H), BF16), v((W, W), BF16)]
+        + [v((2, ZB, H), BF16), v((2, W, H), BF16)]
         + [v((NT, ZB, H), BF16), v((NT, ZB, H), BF16), v((ZB, H), F32), v((CB, H), F32), v((CB, W), F32)]
-        + [v((TOK, W), BF16), v((NT, TB, W), BF16), v((TB, W), BF16), v((TOK, W), BF16), v((W, TOK), BF16)]
+        + [v((TOK, W), BF16), v((NT, TB, W), BF16), v((TOK, W), BF16), v((W, TOK), BF16)]
         + scatter_scratch()
         + [v((ZB, H), F32), v((CB, H), F32), v((CB, W), F32)]
         + [v((ER, W), BF16), v((TOK, W), BF16), v((TOK, W), BF16), v((ER, W), F32)]
@@ -489,7 +612,7 @@
         in_specs=[hbm] * 5,
         out_specs=[hbm] * 5,
         scratch_shapes=[v(a.shape, a.dtype) for a in shapes]
-        + [pltpu.SemaphoreType.DMA((5,))] * 2,
+        + [pltpu.SemaphoreType.DMA((9,))] * 2,
         compiler_params=pltpu.CompilerParams(vmem_limit_bytes=VMEM_LIMIT),
     )(*results)
     return decoded, grad_attended, weight_t.T, encoder_t.T, grad_decoder

time: 79.7 us -> 77.4 us (0.971)
  Pallas kernels: 78.9 us -> 76.6 us
    pallas_call x1, Pallas kernels: 76.4 us -> 74.3 us  [body(): pl.pallas_call(kernel, out_shape=shapes, in_specs=[hbm] * 5, out_specs=[h...]
where the time goes in v3:
time: 77.4 us; the launch traced here: 77.3 us
  Pallas kernels  76.6 us (99%)
    pallas_call x1, Pallas kernels, body(): pl.pallas_call(kernel, out_shape=shapes, in_specs=[hbm] * 5, out_specs=[h...  74.3 us
    pallas_call x1, Pallas kernels, body(): pl.pallas_call(hand_on, out_shape=shapes, in_specs=[hbm] * 5, out_specs=[...  2.29 us

profile of v3, /device:TPU:1, one launch (start us, length us, event | category | flops | bytes accessed | tf_op | source)
XLA Modules:
  0.0 77.3 jit_solution(7819130609755725899)
XLA Ops:
  0.6 74.3 %shard_map.92 = (bf16[256,768]{1,0:T(8,128)(2,1)}, bf16[256,768]{1,0:T(8,128)(2,1)}, f32[192,768]{1,0:T(8,128)}, f32[24,768]{1,0:T(8,128)}, f32[24,768]{1,0:T(8,128)}) custom-call(bf16[256,768]{1,0:T(8,128)(2,1)} %att_h.1, bf16[768,6144]{1,0:T(8,128)(2,1)} %w_h.1, bf16[768,768]{1,0:T(8,128)(2,1)} %enc_h.1, bf16[768,768]{1,0:T(8,128)(2,1)} %dec_h.1, ...), custom_call_target="tpu_custom_call" | custom-call | tf_op jit(solution)/shard_map/pallas_call | solution.py:599
  75.0 2.3 %shard_map.93 = (bf16[256,768]{1,0:T(8,128)(2,1)}, bf16[256,768]{1,0:T(8,128)(2,1)}, f32[192,768]{1,0:T(8,128)}, f32[24,768]{1,0:T(8,128)}, f32[24,768]{1,0:T(8,128)}) custom-call(bf16[256,768]{1,0:T(8,128)(2,1)} %get-tuple-element.15.refs_0_, bf16[256,768]{1,0:T(8,128)(2,1)} %get-tuple-element.16.refs_1_, f32[192,768]{1,0:T(8,128)} %get-tuple-element.17.refs_2_, ...), custom_call_target="tpu_custom_call" | custom-call | tf_op jit(solution)/shard_map/pallas_call | solution.py:609

commit v4 on v3

--- a/solution.py
+++ b/solution.py
@@ -27,9 +27,9 @@
 TG = True
 SORD = True
 GCPOS = 2
-MYP = 1
-MZP = 1
-MGP = 1
+GO = 1
+ZE = 1
+MC = 0
 
 
 def mm(a, b, ca, cb):
@@ -413,7 +413,7 @@
     kt[c, yz_rows(y, z)] = (kacc[:, me_h] + krcv[...].astype(F32)).astype(BF16)
     kg = Gather(kt)
     kg.start()
-    if GCPOS < 2:
+    if GO == 1:
         gcf[rows(t, TB), :] = chunk_sum(gcs, gcr, gc_in)
         gcg.start()
         kg.z_step(1)
@@ -426,73 +426,65 @@
         kg.z_step(3)
         kg.z_step(2)
         kg.own_row()
-        step(6)
         gcf[rows(t, TB), :] = chunk_sum(gcs, gcr, gc_in)
         gcg.start()
         gcg.mid()
     step(7)
 
-    l_att.wait()
-    ms = Scatter(gct, att, (m0, m1, m2, m3, m4, m5, m6, m7))
-    if MYP == 0:
-        gcg.end()
-        gct[...] = gcf[...].T
-        ms.core_start()
-        ms.core_own()
-        ms.y_start()
     kg.y_step(1)
     kg.y_step(3)
-    if MYP >= 1:
-        gcg.end()
-        gct[...] = gcf[...].T
-        ms.core_start()
     kg.y_step(2)
-    if MYP == 1:
-        ms.core_own()
-    if MYP == 2:
-        ms.core_own()
-        ms.y_start()
     kg.finish()
-    step(0)
-
+
+    l_att.wait()
     cws[...] = (mm(att[:, :H], kt[0], 1, 1) + mm(att[:, H:], kt[1], 1, 1)).astype(BF16)
     cw_in = {
         k: send(cws.at[rows(t_to(k), TB), :], cwr.at[k], {"tensor": t_to(k)}) for k in order
     }
-    if MYP == 1:
-        ms.y_start()
+    gcg.end()
+    step(9)
+    gct[...] = gcf[...].T
+    ms = Scatter(gct, att, (m0, m1, m2, m3, m4, m5, m6, m7))
+    ms.core_start()
+    ms.core_own()
+    ms.y_start()
     ga_v[:, :H] = mm(gcf[...], kt[0], 1, 0).astype(BF16)
     ga_v[:, H:] = mm(gcf[...], kt[1], 1, 0).astype(BF16)
     o_ga = local(ga_v, ga_out)
-    if MZP == 0:
-        ms.z_start()
     cwf[rows(t, TB), :] = chunk_sum(cws, cwr, cw_in)
     cwg = TensorGather(lambda tt: cwf.at[rows(tt, TB), :])
     cwg.start()
-    if MZP == 1:
-        ms.z_start()
-    cwg.mid()
+    if MC == 0:
+        cwg.mid()
+    ms.z_start()
+    if MC == 1:
+        cwg.mid()
     step(1)
-    if MZP == 2:
-        ms.z_start()
-    m_block = ms.z_end().astype(BF16)
-    mt[c, yz_rows(y, z)] = m_block
-    mch[c] = m_block
-    m_core = send(mch.at[c], mch.at[c], other)
     mg = Gather(mt)
-    mg.start()
+
+    def m_done():
+        m_block = ms.z_end().astype(BF16)
+        mt[c, yz_rows(y, z)] = m_block
+        mch[c] = m_block
+        mg.m_core = send(mch.at[c], mch.at[c], other)
+        mg.start()
+
+    if ZE == 0:
+        m_done()
     cwg.end()
     step(2)
     cwt[...] = cwf[...].T
     ds = Scatter(cwt, go, (d0, d1, d2, d3, d4, d5, d6, d7))
     ds.core_start()
+    if ZE == 1:
+        m_done()
     ds.core_own()
-    if MGP == 0:
-        mg.z_step(1)
-        mg.z_step(3)
     ds.y_start()
+    if ZE == 2:
+        m_done()
+    step(10)
     g_in = {}
-    m_core.wait_recv()
+    mg.m_core.wait_recv()
     for k in order + (0,):
         val = mm(mch[0], wv[t_to(k), :H, :], 1, 0) + mm(mch[1], wv[t_to(k), H:, :], 1, 0)
         if k:
@@ -501,9 +493,8 @@
         else:
             gsum[...] = val
     step(8)
-    if MGP == 1:
-        mg.z_step(1)
-        mg.z_step(3)
+    mg.z_step(1)
+    mg.z_step(3)
     mg.z_step(2)
     mg.own_row()
     dec_v[...] = mm(cwf[...], dec[...], 1, 0).astype(BF16)

time: 77.4 us -> 75.4 us (0.974)
  Pallas kernels: 76.6 us -> 74.6 us
    pallas_call x1, Pallas kernels: 74.3 us -> 72.3 us  [body(): pl.pallas_call(kernel, out_shape=shapes, in_specs=[hbm] * 5, out_specs=[h...]
where the time goes in v4:
time: 75.4 us; the launch traced here: 75.3 us
  Pallas kernels  74.6 us (99%)
    pallas_call x1, Pallas kernels, body(): pl.pallas_call(kernel, out_shape=shapes, in_specs=[hbm] * 5, out_specs=[h...  72.3 us
    pallas_call x1, Pallas kernels, body(): pl.pallas_call(hand_on, out_shape=shapes, in_specs=[hbm] * 5, out_specs=[...  2.29 us

profile of v4, /device:TPU:1, one launch (start us, length us, event | category | flops | bytes accessed | tf_op | source)
XLA Modules:
  0.0 75.3 jit_solution(7577757603004477944)
XLA Ops:
  0.6 72.3 %shard_map.92 = (bf16[256,768]{1,0:T(8,128)(2,1)}, bf16[256,768]{1,0:T(8,128)(2,1)}, f32[192,768]{1,0:T(8,128)}, f32[24,768]{1,0:T(8,128)}, f32[24,768]{1,0:T(8,128)}) custom-call(bf16[256,768]{1,0:T(8,128)(2,1)} %att_h.1, bf16[768,6144]{1,0:T(8,128)(2,1)} %w_h.1, bf16[768,768]{1,0:T(8,128)(2,1)} %enc_h.1, bf16[768,768]{1,0:T(8,128)(2,1)} %dec_h.1, ...), custom_call_target="tpu_custom_call" | custom-call | tf_op jit(solution)/shard_map/pallas_call | solution.py:590
  73.0 2.3 %shard_map.93 = (bf16[256,768]{1,0:T(8,128)(2,1)}, bf16[256,768]{1,0:T(8,128)(2,1)}, f32[192,768]{1,0:T(8,128)}, f32[24,768]{1,0:T(8,128)}, f32[24,768]{1,0:T(8,128)}) custom-call(bf16[256,768]{1,0:T(8,128)(2,1)} %get-tuple-element.15.refs_0_, bf16[256,768]{1,0:T(8,128)(2,1)} %get-tuple-element.16.refs_1_, f32[192,768]{1,0:T(8,128)} %get-tuple-element.17.refs_2_, ...), custom_call_target="tpu_custom_call" | custom-call | tf_op jit(solution)/shard_map/pallas_call | solution.py:600

commit v5 on v4

--- a/solution.py
+++ b/solution.py
@@ -19,7 +19,7 @@
 ER = W // 4
 SCALE = 1.0 / float(8192) ** 0.5
 N_COPIES = 140
-VMEM_LIMIT = 62 * 1024 * 1024
+VMEM_LIMIT = 60 * 1024 * 1024
 T1 = 7
 T2 = 2
 T3 = 3
@@ -43,10 +43,10 @@
     gcs, gcr, gcf, gct,
     etr, kacc, ksnd, krcv, kt,
     m0, m1, m2, m3, m4, m5, m6, m7, mch, mt,
-    gs, gr, gsum, gswp, ge_v,
+    gs, gr, gsum, gswp,
     cws, cwr, cwf, cwt,
-    d0, d1, d2, d3, d4, d5, d6, d7, dsum, dswp, gd_v,
-    erow, dec_v, ga_v, gw_v,
+    d0, d1, d2, d3, d4, d5, d6, d7, dsum, dswp,
+    erow,
     lsem, ssem, rsem,
 ):
     d = lax.axis_index("dp")
@@ -448,9 +448,8 @@
     ms.core_start()
     ms.core_own()
     ms.y_start()
-    ga_v[:, :H] = mm(gcf[...], kt[0], 1, 0).astype(BF16)
-    ga_v[:, H:] = mm(gcf[...], kt[1], 1, 0).astype(BF16)
-    o_ga = local(ga_v, ga_out)
+    ga_out[:, :H] = mm(gcf[...], kt[0], 1, 0).astype(BF16)
+    ga_out[:, H:] = mm(gcf[...], kt[1], 1, 0).astype(BF16)
     cwf[rows(t, TB), :] = chunk_sum(cws, cwr, cw_in)
     cwg = TensorGather(lambda tt: cwf.at[rows(tt, TB), :])
     cwg.start()
@@ -497,8 +496,7 @@
     mg.z_step(3)
     mg.z_step(2)
     mg.own_row()
-    dec_v[...] = mm(cwf[...], dec[...], 1, 0).astype(BF16)
-    o_dec = local(dec_v, dec_out)
+    dec_out[...] = mm(cwf[...], dec[...], 1, 0).astype(BF16)
     step(3)
     ds.zc = {}
     ds.z_sum(2)
@@ -514,41 +512,28 @@
     mg.y_step(2)
     step(4)
     g_core.wait_recv()
-    ge_v[:, me_h] = SCALE * gsum[rows(c, CB), :]
-    ge_v[:, ot_h] = SCALE * gswp[...]
-    o_ge = local(ge_v, ge_out)
+    ge_out[:, me_h] = SCALE * gsum[rows(c, CB), :]
+    ge_out[:, ot_h] = SCALE * gswp[...]
     dsum[...] = ds.z_end()
     d_core = send(dsum.at[rows(1 - c, CB), :], dswp, other)
     mg.finish()
-    gw_v[:, :H] = SCALE * mm(erow[...], mt[0], 1, 0)
-    gw_v[:, H:] = SCALE * mm(erow[...], mt[1], 1, 0)
-    o_gw = local(gw_v, gw_out)
-    gd_v[:, me_h] = SCALE * dsum[rows(c, CB), :]
+    gw_out[:, :H] = SCALE * mm(erow[...], mt[0], 1, 0)
+    gw_out[:, H:] = SCALE * mm(erow[...], mt[1], 1, 0)
+    gd_out[:, me_h] = SCALE * dsum[rows(c, CB), :]
     d_core.wait_recv()
-    gd_v[:, ot_h] = SCALE * dswp[...]
-    o_gd = local(gd_v, gd_out)
+    gd_out[:, ot_h] = SCALE * dswp[...]
 
     for cp in sent:
         cp.wait_send()
     tree.drain()
-    for cp in (o_ga, o_dec, o_gw, o_ge, o_gd):
-        cp.wait()
     assert counter[0] <= N_COPIES, counter
 
 
 def hand_on(*refs):
-    ins, outs, held, sem_in, sem_out = refs[:5], refs[5:10], refs[10:15], refs[15], refs[16]
-    pieces = [(2, slice(i * 64, i * 64 + 64)) for i in range(3)]
-    pieces += [(a, slice(i * 128, i * 128 + 128)) for a in (0, 1) for i in range(2)]
-    pieces += [(a, slice(0, CB)) for a in (3, 4)]
-    first = [pltpu.make_async_copy(ins[a].at[r], held[a].at[r], sem_in.at[i]) for i, (a, r) in enumerate(pieces)]
-    second = [pltpu.make_async_copy(held[a].at[r], outs[a].at[r], sem_out.at[i]) for i, (a, r) in enumerate(pieces)]
-    for cp in first:
+    copies = [pltpu.make_async_copy(refs[i], refs[5 + i], refs[10].at[i]) for i in range(5)]
+    for cp in copies:
         cp.start()
-    for one, two in zip(first, second):
-        one.wait()
-        two.start()
-    for cp in second:
+    for cp in copies:
         cp.wait()
 
 
@@ -568,11 +553,11 @@
         + [v((NT, ZB, H), BF16), v((ZB, W), F32), v((ZB, H), BF16), v((ZB, H), BF16), v((2, W, H), BF16)]
         + scatter_scratch()
         + [v((2, ZB, H), BF16), v((2, W, H), BF16)]
-        + [v((NT, ZB, H), BF16), v((NT, ZB, H), BF16), v((ZB, H), F32), v((CB, H), F32), v((CB, W), F32)]
+        + [v((NT, ZB, H), BF16), v((NT, ZB, H), BF16), v((ZB, H), F32), v((CB, H), F32)]
         + [v((TOK, W), BF16), v((NT, TB, W), BF16), v((TOK, W), BF16), v((W, TOK), BF16)]
         + scatter_scratch()
-        + [v((ZB, H), F32), v((CB, H), F32), v((CB, W), F32)]
-        + [v((ER, W), BF16), v((TOK, W), BF16), v((TOK, W), BF16), v((ER, W), F32)]
+        + [v((ZB, H), F32), v((CB, H), F32)]
+        + [v((ER, W), BF16)]
         + [
             pltpu.SemaphoreType.DMA((20,)),
             pltpu.SemaphoreType.DMA((N_COPIES,)),
@@ -589,9 +574,9 @@
     )
     results = pl.pallas_call(
         kernel,
-        out_shape=shapes,
+        out_shape=tuple(pltpu.VMEM(a.shape, a.dtype) for a in shapes),
         in_specs=[hbm] * 5,
-        out_specs=[hbm] * 5,
+        out_specs=[pl.BlockSpec(memory_space=pltpu.VMEM)] * 5,
         scratch_shapes=scratch,
         compiler_params=pltpu.CompilerParams(
             collective_id=0, has_side_effects=True, vmem_limit_bytes=VMEM_LIMIT
@@ -600,11 +585,10 @@
     decoded, grad_attended, weight_t, encoder_t, grad_decoder = pl.pallas_call(
         hand_on,
         out_shape=shapes,
-        in_specs=[hbm] * 5,
+        in_specs=[pl.BlockSpec(memory_space=pltpu.VMEM)] * 5,
         out_specs=[hbm] * 5,
-        scratch_shapes=[v(a.shape, a.dtype) for a in shapes]
-        + [pltpu.SemaphoreType.DMA((9,))] * 2,
-        compiler_params=pltpu.CompilerParams(vmem_limit_bytes=VMEM_LIMIT),
+        scratch_shapes=[pltpu.SemaphoreType.DMA((5,))],
+        compiler_params=pltpu.CompilerParams(vmem_limit_bytes=32 * 1024 * 1024),
     )(*results)
     return decoded, grad_attended, weight_t.T, encoder_t.T, grad_decoder
 

time: 75.4 us -> 73.7 us (0.977)
  Pallas kernels: 74.6 us -> 72.9 us
    pallas_call x2, Pallas kernels: 74.6 us -> 72.9 us  [the longest x1 71.7 us: body(): pl.pallas_call(kernel, out_shape=tuple((pltpu.VMEM(a.shape, a.dtype) for...]
where the time goes in v5:
time: 73.7 us; the launch traced here: 73.5 us
  Pallas kernels  72.9 us (99%)
    pallas_call x1, Pallas kernels, body(): pl.pallas_call(kernel, out_shape=tuple((pltpu.VMEM(a.shape, a.dtype) for...  71.7 us

profile of v5, /device:TPU:1, one launch (start us, length us, event | category | flops | bytes accessed | tf_op | source)
XLA Modules:
  0.0 73.5 jit_solution(12102287712777835469)
XLA Ops:
  0.6 71.7 %shard_map.92 = (bf16[256,768]{1,0:T(8,128)(2,1)S(1)}, bf16[256,768]{1,0:T(8,128)(2,1)S(1)}, f32[192,768]{1,0:T(8,128)S(1)}, f32[24,768]{1,0:T(8,128)S(1)}, f32[24,768]{1,0:T(8,128)S(1)}) custom-call(bf16[256,768]{1,0:T(8,128)(2,1)} %att_h.1, bf16[768,6144]{1,0:T(8,128)(2,1)} %w_h.1, bf16[768,768]{1,0:T(8,128)(2,1)} %enc_h.1, bf16[768,768]{1,0:T(8,128)(2,1)} %dec_h.1, ...), custom_call_target="tpu_custom_call" | custom-call | tf_op jit(solution)/shard_map/pallas_call | solution.py:575
  72.3 1.2 %shard_map.93 = (bf16[256,768]{1,0:T(8,128)(2,1)}, bf16[256,768]{1,0:T(8,128)(2,1)}, f32[192,768]{1,0:T(8,128)}, f32[24,768]{1,0:T(8,128)}, f32[24,768]{1,0:T(8,128)}) custom-call(bf16[256,768]{1,0:T(8,128)(2,1)S(1)} %get-tuple-element.15.refs_0_, bf16[256,768]{1,0:T(8,128)(2,1)S(1)} %get-tuple-element.16.refs_1_, f32[192,768]{1,0:T(8,128)S(1)} %get-tuple-element.17.refs_2_, ...), custom_call_target="tpu_custom_call" | custom-call | tf_op jit(solution)/shard_map/pallas_call | solution.py:585

commit v6 on v5

--- a/solution.py
+++ b/solution.py
@@ -30,6 +30,7 @@
 GO = 1
 ZE = 1
 MC = 0
+FL = True
 
 
 def mm(a, b, ca, cb):
@@ -108,6 +109,17 @@
         cp.start()
         sent.append(cp)
         return cp
+
+    marks = []
+
+    def mark():
+        marks.append(len(sent))
+
+    def flush():
+        if FL:
+            for cp in sent[: marks[-1]]:
+                cp.wait_send()
+            del sent[: marks[-1]]
 
     lcount = [0]
 
@@ -470,6 +482,7 @@
 
     if ZE == 0:
         m_done()
+    mark()
     cwg.end()
     step(2)
     cwt[...] = cwf[...].T
@@ -491,7 +504,7 @@
             g_in[k] = send(gs.at[k], gr.at[k], {"tensor": t_to(k)})
         else:
             gsum[...] = val
-    step(8)
+    flush()
     mg.z_step(1)
     mg.z_step(3)
     mg.z_step(2)
@@ -504,9 +517,11 @@
         g_in[k].wait_recv()
         gsum[...] += gr[k].astype(F32)
     g_core = send(gsum.at[rows(1 - c, CB), :], gswp, other)
+    mark()
     ds.z_sum(1)
     ds.z_sum(3)
     ds.z_sum(0)
+    flush()
     mg.y_step(1)
     mg.y_step(3)
     mg.y_step(2)

time: 73.7 us -> 73.5 us (level)
  no operation moved by 1% of the time
where the time goes in v6:
time: 73.5 us; the launch traced here: 73.3 us
  Pallas kernels  72.7 us (99%)
    pallas_call x1, Pallas kernels, body(): pl.pallas_call(kernel, out_shape=tuple((pltpu.VMEM(a.shape, a.dtype) for...  71.5 us

profile of v6, /device:TPU:1, one launch (start us, length us, event | category | flops | bytes accessed | tf_op | source)
XLA Modules:
  0.0 73.3 jit_solution(13443198989633234430)
XLA Ops:
  0.6 71.5 %shard_map.92 = (bf16[256,768]{1,0:T(8,128)(2,1)S(1)}, bf16[256,768]{1,0:T(8,128)(2,1)S(1)}, f32[192,768]{1,0:T(8,128)S(1)}, f32[24,768]{1,0:T(8,128)S(1)}, f32[24,768]{1,0:T(8,128)S(1)}) custom-call(bf16[256,768]{1,0:T(8,128)(2,1)} %att_h.1, bf16[768,6144]{1,0:T(8,128)(2,1)} %w_h.1, bf16[768,768]{1,0:T(8,128)(2,1)} %enc_h.1, bf16[768,768]{1,0:T(8,128)(2,1)} %dec_h.1, ...), custom_call_target="tpu_custom_call" | custom-call | tf_op jit(solution)/shard_map/pallas_call | solution.py:590
  72.2 1.2 %shard_map.93 = (bf16[256,768]{1,0:T(8,128)(2,1)}, bf16[256,768]{1,0:T(8,128)(2,1)}, f32[192,768]{1,0:T(8,128)}, f32[24,768]{1,0:T(8,128)}, f32[24,768]{1,0:T(8,128)}) custom-call(bf16[256,768]{1,0:T(8,128)(2,1)S(1)} %get-tuple-element.15.refs_0_, bf16[256,768]{1,0:T(8,128)(2,1)S(1)} %get-tuple-element.16.refs_1_, f32[192,768]{1,0:T(8,128)S(1)} %get-tuple-element.17.refs_2_, ...), custom_call_target="tpu_custom_call" | custom-call | tf_op jit(solution)/shard_map/pallas_call | solution.py:600

commit v7 on v6

--- a/solution.py
+++ b/solution.py
@@ -449,10 +449,12 @@
     kg.finish()
 
     l_att.wait()
-    cws[...] = (mm(att[:, :H], kt[0], 1, 1) + mm(att[:, H:], kt[1], 1, 1)).astype(BF16)
-    cw_in = {
-        k: send(cws.at[rows(t_to(k), TB), :], cwr.at[k], {"tensor": t_to(k)}) for k in order
-    }
+    cw_in = {}
+    for side, ks in ((1 - zl, (6, 5, 7, 4)), (zl, (2, 1, 3))):
+        r = rows(side, TOK // 2)
+        cws[r, :] = (mm(att[r, :H], kt[0], 1, 1) + mm(att[r, H:], kt[1], 1, 1)).astype(BF16)
+        for k in ks:
+            cw_in[k] = send(cws.at[rows(t_to(k), TB), :], cwr.at[k], {"tensor": t_to(k)})
     gcg.end()
     step(9)
     gct[...] = gcf[...].T

time: 73.5 us -> 72.6 us (0.988)
  Pallas kernels: 72.7 us -> 71.8 us
    pallas_call x1, Pallas kernels: 71.5 us -> 70.7 us  [body(): pl.pallas_call(kernel, out_shape=tuple((pltpu.VMEM(a.shape, a.dtype) for...]
where the time goes in v7:
time: 72.6 us; the launch traced here: 72.5 us
  Pallas kernels  71.8 us (99%)
    pallas_call x1, Pallas kernels, body(): pl.pallas_call(kernel, out_shape=tuple((pltpu.VMEM(a.shape, a.dtype) for...  70.7 us

profile of v7, /device:TPU:1, one launch (start us, length us, event | category | flops | bytes accessed | tf_op | source)
XLA Modules:
  0.0 72.5 jit_solution(18427327343577219427)
XLA Ops:
  0.6 70.7 %shard_map.92 = (bf16[256,768]{1,0:T(8,128)(2,1)S(1)}, bf16[256,768]{1,0:T(8,128)(2,1)S(1)}, f32[192,768]{1,0:T(8,128)S(1)}, f32[24,768]{1,0:T(8,128)S(1)}, f32[24,768]{1,0:T(8,128)S(1)}) custom-call(bf16[256,768]{1,0:T(8,128)(2,1)} %att_h.1, bf16[768,6144]{1,0:T(8,128)(2,1)} %w_h.1, bf16[768,768]{1,0:T(8,128)(2,1)} %enc_h.1, bf16[768,768]{1,0:T(8,128)(2,1)} %dec_h.1, ...), custom_call_target="tpu_custom_call" | custom-call | tf_op jit(solution)/shard_map/pallas_call | solution.py:592
  71.3 1.2 %shard_map.93 = (bf16[256,768]{1,0:T(8,128)(2,1)}, bf16[256,768]{1,0:T(8,128)(2,1)}, f32[192,768]{1,0:T(8,128)}, f32[24,768]{1,0:T(8,128)}, f32[24,768]{1,0:T(8,128)}) custom-call(bf16[256,768]{1,0:T(8,128)(2,1)S(1)} %get-tuple-element.15.refs_0_, bf16[256,768]{1,0:T(8,128)(2,1)S(1)} %get-tuple-element.16.refs_1_, f32[192,768]{1,0:T(8,128)S(1)} %get-tuple-element.17.refs_2_, ...), custom_call_target="tpu_custom_call" | custom-call | tf_op jit(solution)/shard_map/pallas_call | solution.py:602
